TPU v7x, 512 devices: a whole 4x4x16 slice. The times are simulated.
512 devices in a mesh: row: 64 (over y_lo, z, core), grp: 8 (over y_hi, x).
Axes of the slice: x: 4, y: 4 (y_hi: 2, y_lo: 2; y = y_hi * 2 + y_lo), z: 16, core: 2. Of those that a mesh axis runs over, the one named last changes fastest.
Arguments:
- pair: bfloat16 [448, 448, 128], P('row', 'grp'), may hold values from -6 to 6
- pair_mask: int32 [448, 448], P('row', 'grp'), may hold values 0 or 1
- w_ab: bfloat16 [2, 128, 512], replicated, may hold values from -0.5 to 0.5
- w_gate: bfloat16 [2, 128, 128], replicated, may hold values from -0.5 to 0.5
- w_out: bfloat16 [2, 128, 128], replicated, may hold values from -0.5 to 0.5
Outputs:
- pair_out: bfloat16 [448, 448, 128], P('row', 'grp')
All inputs are finite; a program needn't handle non-finite values. No bound on the sum of `pair_mask` on one device may be relied on, other than what follows from the above.
Results may differ from a plain program's by a relative error of at most 0.017.
Values may be sent and summed in bfloat16 or wider, within the bound.
A program may use at most 64 MiB of HBM per device.

v0:
```python
import jax
import jax.numpy as jnp
from jax import lax
from jax.sharding import PartitionSpec as P


def normalize(values, axis):
    mean = jnp.mean(values, axis=axis, keepdims=True)
    centered = values - mean
    var = jnp.mean(centered * centered, axis=axis, keepdims=True)
    return centered * lax.rsqrt(var + 1e-05)


def prepare(pair, keep, w_ab, w_gate):
    width = pair.shape[2]
    normed = normalize(pair.astype(jnp.float32), 2).astype(jnp.bfloat16)
    proj = jnp.einsum("rmc,cf->frm", normed, w_ab, preferred_element_type=jnp.float32)
    left = (jax.nn.sigmoid(proj[:width]) * proj[width : 2 * width] * keep).astype(jnp.bfloat16)
    right = (jax.nn.sigmoid(proj[2 * width : 3 * width]) * proj[3 * width :] * keep).astype(
        jnp.bfloat16
    )
    gate = jax.nn.sigmoid(
        jnp.einsum("rmc,cd->rmd", normed, w_gate, preferred_element_type=jnp.float32)
    )
    return (left, right, gate)


def finish(pair, gate, sums, w_out):
    tnorm = normalize(sums.astype(jnp.float32), 0).astype(jnp.bfloat16)
    out = jnp.einsum("crm,cd->rmd", tnorm, w_out, preferred_element_type=jnp.float32)
    return (pair.astype(jnp.float32) + gate * out).astype(jnp.bfloat16)


def body(pair, pair_mask, w_ab, w_gate, w_out):
    keep = pair_mask.astype(jnp.float32)
    left, right, gate = prepare(pair, keep, w_ab[0], w_gate[0])
    left, right = (
        lax.all_to_all(left, "grp", split_axis=0, concat_axis=2, tiled=True),
        lax.all_to_all(right, "grp", split_axis=0, concat_axis=2, tiled=True),
    )
    sums = jnp.einsum(
        "cik,cjk->cij",
        left,
        lax.all_gather(right, "row", axis=1, tiled=True),
        preferred_element_type=jnp.float32,
    ).astype(jnp.bfloat16)
    sums = lax.all_to_all(sums, "grp", split_axis=2, concat_axis=0, tiled=True)
    middle = finish(pair, gate, sums, w_out[0])
    left, right, gate = prepare(middle, keep, w_ab[1], w_gate[1])
    left, right = (
        lax.all_to_all(left, "grp", split_axis=0, concat_axis=2, tiled=True),
        lax.all_to_all(right, "grp", split_axis=0, concat_axis=2, tiled=True),
    )
    turned = lax.all_to_all(left, "row", split_axis=2, concat_axis=1, tiled=True)
    sums = jnp.einsum(
        "cki,ckj->cij",
        turned,
        lax.all_gather(right, "row", axis=1, tiled=True),
        preferred_element_type=jnp.float32,
    ).astype(jnp.bfloat16)
    sums = lax.all_to_all(sums, "grp", split_axis=2, concat_axis=0, tiled=True)
    return finish(middle, gate, sums, w_out[1])


def solution(mesh):
    return jax.shard_map(
        body,
        mesh=mesh,
        in_specs=(P("row", "grp", None), P("row", "grp"), P(), P(), P()),
        out_specs=P("row", "grp", None),
        check_vma=False,
    )
```

profile of v0, /device:TPU:24, one launch (start us, length us, event | category | flops | bytes accessed | tf_op | source)
XLA Modules:
  0.0 357.4 jit_solution(16314847999409305105)
XLA Ops:
  6.5 1.0 convert_reduce_fusion
  7.6 1.1 fusion.23
  8.7 0.7 convert_element_type.79
  9.4 1.3 convolution_bitcast_fusion.1
  11.1 0.4 reshape.67
  11.4 12.0 %all_to_all.108 = bf16[8,2,3136]{2,1,0:T(2,128)(2,1)S(1)} all-to-all(bf16[8,2,3136]{2,1,0:T(2,128)(2,1)S(1)} %reshape.67), channel_id=1, replica_groups=mesh['row'=64,'grp'=8] {'grp'}, dimensions={0} | all-to-all | bytes 200704 | tf_op jit(solution)/shard_map/all_to_all | solution.py:39
  23.5 0.4 reshape.68
  24.0 0.8 all_to_all.86
  25.1 0.4 reshape.65
  25.4 10.8 %all_to_all.109 = bf16[8,2,3136]{2,1,0:T(2,128)(2,1)S(1)} all-to-all(bf16[8,2,3136]{2,1,0:T(2,128)(2,1)S(1)} %reshape.65), channel_id=1, replica_groups=mesh['row'=64,'grp'=8] {'grp'}, dimensions={0} | all-to-all | bytes 200704 | tf_op jit(solution)/shard_map/all_to_all | solution.py:38
  36.2 0.4 reshape.66
  36.7 0.2 reshape.63
  37.0 118.6 %all-gather.3.cloned.1.call-done = bf16[16,448,448]{2,0,1:T(8,128)(2,1)} async-done(((bf16[16,7,448]{2,0,1:T(8,128)(2,1)}), bf16[16,448,448]{2,0,1:T(8,128)(2,1)}) %all-gather.3.cloned.1.call-update) | async-done | bytes 6422544 | tf_op jit(solution)/shard_map/all_gather | solution.py:44
  155.6 10.8 %fusion.12 = bf16[16,7,448]{2,1,0:T(8,128)(2,1)S(1)} fusion(bf16[16,7,448]{2,1,0:T(8,128)(2,1)S(1)} %reshape.63, bf16[16,448,448]{2,0,1:T(8,128)(2,1)} %all-gather.3.cloned.1.call-done), kind=kOutput, calls=%fused_computation.18 | convolution fusion | flops 45007872 | bytes 6623232 | tf_op jit(solution)/shard_map/cik,cjk->cij/dot_general | solution.py:41
  166.4 0.6 copy.93
  167.0 1.4 reshape.69
  168.4 7.1 %all-to-all-start.2 = ((bf16[8,2,3136]{2,1,0:T(2,128)(2,1)}), bf16[8,2,3136]{2,1,0:T(2,128)(2,1)S(1)}, u32[]{:S(2)}, u32[]{:S(2)}) async-start(bf16[8,2,3136]{2,1,0:T(2,128)(2,1)} %reshape.69), calls=%async_computation.2 | async-start | bytes 204800 | tf_op jit(solution)/shard_map/all_to_all | solution.py:47
  175.5 0.5 all-gather.5.cloned.1.call-start
  176.1 0.3 fusion.11
  176.4 4.1 %all-to-all-done.2 = bf16[8,2,3136]{2,1,0:T(2,128)(2,1)S(1)} async-done(((bf16[8,2,3136]{2,1,0:T(2,128)(2,1)}), bf16[8,2,3136]{2,1,0:T(2,128)(2,1)S(1)}, u32[]{:S(2)}, u32[]{:S(2)}) %all-to-all-start.2) | async-done | bytes 100384 | tf_op jit(solution)/shard_map/all_to_all | solution.py:47
  180.5 0.9 reshape.70
  181.4 0.6 copy.94
  182.4 0.3 fusion.59
  182.8 0.2 multiply_reduce_fusion.2
  183.0 0.3 convolution_bitcast_fusion
  183.7 0.4 reshape.75
  184.1 10.5 %all_to_all.110 = bf16[8,2,3136]{2,1,0:T(2,128)(2,1)S(1)} all-to-all(bf16[8,2,3136]{2,1,0:T(2,128)(2,1)S(1)} %reshape.75), channel_id=1, replica_groups=mesh['row'=64,'grp'=8] {'grp'}, dimensions={0} | all-to-all | bytes 200704 | tf_op jit(solution)/shard_map/all_to_all | solution.py:52
  194.5 0.4 reshape.76
  195.1 0.8 all_to_all.99
  196.2 0.4 reshape.71
  196.5 10.5 %all_to_all.111 = bf16[8,2,3136]{2,1,0:T(2,128)(2,1)S(1)} all-to-all(bf16[8,2,3136]{2,1,0:T(2,128)(2,1)S(1)} %reshape.71), channel_id=1, replica_groups=mesh['row'=64,'grp'=8] {'grp'}, dimensions={0} | all-to-all | bytes 200704 | tf_op jit(solution)/shard_map/all_to_all | solution.py:51
  207.0 0.4 reshape.72
  207.4 0.5 copy.118
  207.9 0.8 reshape.73
  208.8 25.3 %all_to_all.112 = bf16[64,2,392]{2,1,0:T(2,128)(2,1)S(1)} all-to-all(bf16[64,2,392]{2,1,0:T(2,128)(2,1)S(1)} %reshape.73), channel_id=1, replica_groups=mesh['row'=64,'grp'=8] {'row'}, dimensions={0} | all-to-all | bytes 200704 | tf_op jit(solution)/shard_map/all_to_all | solution.py:54
  234.1 0.9 reshape.74
  235.0 4.0 %copy.121 = bf16[16,64,7,7]{2,1,3,0:T(8,128)(2,1)S(1)} copy(bf16[16,64,7,7]{0,2,3,1:T(8,128)(2,1)S(1)} %bitcast.96) | data formatting | bytes 200704 | tf_op jit(solution)/shard_map/all_to_all | solution.py:54
  238.9 3.4 reshape.64
  242.4 78.7 %all-gather.5.cloned.1.call-done = bf16[16,448,448]{2,0,1:T(8,128)(2,1)} async-done(((bf16[16,7,448]{2,0,1:T(8,128)(2,1)}), bf16[16,448,448]{2,0,1:T(8,128)(2,1)}) %all-gather.5.cloned.1.call-update) | async-done | bytes 6422544 | tf_op jit(solution)/shard_map/all_gather | solution.py:58
  321.1 10.8 %fusion.15 = bf16[16,7,448]{2,1,0:T(8,128)(2,1)S(1)} fusion(bf16[16,448,7]{1,2,0:T(8,128)(2,1)S(1)} %reshape.64, bf16[16,448,448]{2,0,1:T(8,128)(2,1)} %all-gather.5.cloned.1.call-done), kind=kOutput, calls=%fused_computation.19 | convolution fusion | flops 45007872 | bytes 6623232 | tf_op jit(solution)/shard_map/cki,ckj->cij/dot_general | solution.py:55
  331.9 0.6 copy.108
  332.5 1.6 reshape.77
  334.1 8.5 %all-to-all-start.6 = ((bf16[8,2,3136]{2,1,0:T(2,128)(2,1)}), bf16[8,2,3136]{2,1,0:T(2,128)(2,1)S(1)}, u32[]{:S(2)}, u32[]{:S(2)}) async-start(bf16[8,2,3136]{2,1,0:T(2,128)(2,1)} %reshape.77), calls=%async_computation.6 | async-start | bytes 204800 | tf_op jit(solution)/shard_map/all_to_all | solution.py:61
  342.6 0.3 fusion.8
  342.9 4.7 %all-to-all-done.6 = bf16[8,2,3136]{2,1,0:T(2,128)(2,1)S(1)} async-done(((bf16[8,2,3136]{2,1,0:T(2,128)(2,1)}), bf16[8,2,3136]{2,1,0:T(2,128)(2,1)S(1)}, u32[]{:S(2)}, u32[]{:S(2)}) %all-to-all-start.6) | async-done | bytes 100384 | tf_op jit(solution)/shard_map/all_to_all | solution.py:61
  347.5 0.9 reshape.78
  348.4 0.6 copy.109
  349.5 0.9 fusion.20
  (38 shorter events, 2.5 us)
Async XLA Ops:
  6.5 149.1 %all-gather.3.cloned.1.call-start = ((), (), s32[]{:S(2)}) async-start(), calls=%async_computation.7 | async-start | bytes 7454720 | tf_op jit(solution)/shard_map/all_gather | solution.py:44
  10.8 165.2 %copy-start = (bf16[7,56,128]{2,1,0:T(8,128)(2,1)S(1)}, bf16[7,56,128]{2,1,0:T(8,128)(2,1)}, u32[]{:S(2)}) copy-start(bf16[7,56,128]{2,1,0:T(8,128)(2,1)} %param.5) | copy-start | bytes 301060
  10.8 165.2 %copy-start.3 = (bf16[2,128,128]{2,1,0:T(8,128)(2,1)S(1)}, bf16[2,128,128]{2,1,0:T(8,128)(2,1)}, u32[]{:S(2)}) copy-start(bf16[2,128,128]{2,1,0:T(8,128)(2,1)} %param.8) | copy-start | bytes 196612
  37.0 145.4 %copy-start.2 = (bf16[2,128,128]{2,1,0:T(8,128)(2,1)S(1)}, bf16[2,128,128]{2,1,0:T(8,128)(2,1)}, u32[]{:S(2)}) copy-start(bf16[2,128,128]{2,1,0:T(8,128)(2,1)} %param.9) | copy-start | bytes 196612
  37.0 146.0 %copy-start.1 = (bf16[2,128,512]{2,1,0:T(8,128)(2,1)S(1)}, bf16[2,128,512]{2,1,0:T(8,128)(2,1)}, u32[]{:S(2)}) copy-start(bf16[2,128,512]{2,1,0:T(8,128)(2,1)} %param.7) | copy-start | bytes 786436
  168.4 12.1 %all-to-all-start.2 = ((bf16[8,2,3136]{2,1,0:T(2,128)(2,1)}), bf16[8,2,3136]{2,1,0:T(2,128)(2,1)S(1)}, u32[]{:S(2)}, u32[]{:S(2)}) async-start(bf16[8,2,3136]{2,1,0:T(2,128)(2,1)} %reshape.69), calls=%async_computation.2 | async-start | bytes 204800 | tf_op jit(solution)/shard_map/all_to_all | solution.py:47
  175.5 145.6 %all-gather.5.cloned.1.call-start = ((), (), s32[]{:S(2)}) async-start(), calls=%async_computation.8 | async-start | bytes 7454720 | tf_op jit(solution)/shard_map/all_gather | solution.py:58
  334.1 13.5 %all-to-all-start.6 = ((bf16[8,2,3136]{2,1,0:T(2,128)(2,1)}), bf16[8,2,3136]{2,1,0:T(2,128)(2,1)S(1)}, u32[]{:S(2)}, u32[]{:S(2)}) async-start(bf16[8,2,3136]{2,1,0:T(2,128)(2,1)} %reshape.77), calls=%async_computation.6 | async-start | bytes 204800 | tf_op jit(solution)/shard_map/all_to_all | solution.py:61
Sparse Core Ops, SparseCore 0:
  25.0 130.5 all-gather.2
  196.1 124.9 all-gather.4
where the time goes:
time: 363 us; the launch traced here: 357 us
  waiting for transfers between devices  206 us (57%)
  blocking collectives  69.1 us (19%)
  matrix products  25 us (7%)
  local copies, waits for them, and re-layouts  23.3 us (6%)
  starting transfers between devices  16.1 us (4%)
  between operations  14.1 us (4%)
  other arithmetic  3.72 us (1%)
    all_gather x2, waiting for transfers between devices, body(): lax.all_gather(right, 'row', axis=1, tiled=True)  197 us
    all_to_all x1, blocking collectives, body(): lax.all_to_all(left, 'row', split_axis=2, concat_axis=1, tiled=True)  25.3 us
    all_to_all x2, blocking collectives, body(): lax.all_to_all(right, 'grp', split_axis=0, concat_axis=2, tiled=True)  22.5 us
    all_to_all x2, blocking collectives, body(): lax.all_to_all(left, 'grp', split_axis=0, concat_axis=2, tiled=True)  21.2 us
    all_to_all x2, starting transfers between devices, body(): sums = lax.all_to_all(sums, 'grp', split_axis=2, concat_axis=0, tiled=True)  15.6 us
    dot_general x1, matrix products, body(): jnp.einsum('cik,cjk->cij', left, lax.all_gather(right, 'row', axis=1, til...  10.8 us
    dot_general x1, matrix products, body(): jnp.einsum('cki,ckj->cij', turned, lax.all_gather(right, 'row', axis=1, t...  10.8 us
    unnamed x22, local copies, waits for them, and re-layouts  9.4 us
  transfers between devices with their start and end apart: 4, of which 4 were waited for; matrix products, arithmetic and copies ran while one was open for 4% of the time, Pallas kernels for 0%

commit v1 on v0

v1 whole, which is shorter than its diff:
```python
import jax
import jax.numpy as jnp
from jax import lax
from jax.experimental import pallas as pl
from jax.experimental.pallas import tpu as pltpu
from jax.sharding import PartitionSpec as P

MESH = pl.DeviceIdType.MESH
F32, BF16 = jnp.float32, jnp.bfloat16
NZ, NG, ROWS, COLS, RS, MS, CH = 16, 8, 7, 56, 8, 64, 128
TOK = RS * MS
HALF = TOK // 2
AROUND = (8, 7, 9, 6, 10, 5, 11, 4, 12, 3, 13, 2, 14, 1, 15)
EARLY, LATE = 0, 1
F1, F2, MATE, B1, B2, STAGES = 0, 2, 4, 5, 7, 9


def mm(a, b, ca=1, cb=0):
    return lax.dot_general(a, b, (((ca,), (cb,)), ((), ())), preferred_element_type=F32)


def iota2(shape):
    return lax.broadcasted_iota(jnp.int32, shape, 0), lax.broadcasted_iota(jnp.int32, shape, 1)


def one_hot(hit):
    return jnp.where(hit, 1.0, 0.0).astype(BF16)


def normalize(x, axes):
    count = 1
    for a in axes:
        count *= x.shape[a]
    mean = jnp.sum(x, axis=axes, keepdims=True) * (1.0 / count)
    cen = x - mean
    var = jnp.sum(cen * cen, axis=axes, keepdims=True) * (1.0 / count)
    return cen * lax.rsqrt(var + 1e-05)


def sigmoid(x):
    return 0.5 * jnp.tanh(0.5 * x) + 0.5


def swap_halves(a, b):
    low = lax.broadcasted_iota(jnp.int32, a.shape, a.ndim - 1) < 64
    return jnp.where(low, a, pltpu.roll(b, 64, a.ndim - 1)), jnp.where(low, pltpu.roll(a, 64, a.ndim - 1), b)


def kernel(
    pair_hbm, mask_hbm, wab_hbm, wg_hbm, wo_hbm, out_ref,
    pair_ref, mask_ref, wab_ref, wg_ref, wo_ref, wabt, wgt, wot, perm, cols,
    ztok, zt, zn, gate, sides, s1, r1, s2, r2, y0, y1, e0, e1, s3, r3, s4, r4, insem, ssem, rsem,
):
    loads = [
        pltpu.make_async_copy(src, dst, insem.at[n])
        for n, (src, dst) in enumerate(
            ((pair_hbm, pair_ref), (wab_hbm, wab_ref), (mask_hbm, mask_ref), (wg_hbm, wg_ref), (wo_hbm, wo_ref))
        )
    ]
    for load in loads:
        load.start()

    row, g = lax.axis_index("row"), lax.axis_index("grp")
    core = lax.rem(row, 2)
    z = lax.rem(row // 2, NZ)
    yl = row // (2 * NZ)

    mate = 1 - core

    def dev(yl_, z_, core_, g_):
        return (yl_ * (2 * NZ) + z_ * 2 + core_, g_)

    barrier = pltpu.get_barrier_semaphore()

    def greet(device):
        pl.semaphore_signal(barrier, inc=1, device_id=device, device_id_type=MESH)

    for d in AROUND:
        greet(dev(yl, lax.rem(z + d, NZ), core, g))

    def send(src, dst, u, stage, device, is_self=None):
        def remote():
            pltpu.make_async_remote_copy(
                src_ref=src, dst_ref=dst, send_sem=ssem.at[u, stage], recv_sem=rsem.at[u, stage],
                device_id=device, device_id_type=MESH,
            ).start()

        if is_self is None:
            remote()
            return

        @pl.when(is_self)
        def _():
            pltpu.make_async_copy(src, dst, rsem.at[u, stage]).start()

        pl.when(jnp.logical_not(is_self))(remote)

    def send_z(src, dst, u, stage):
        for d in AROUND:
            to = lax.rem(z + d, NZ)
            send(src.at[to], dst.at[z], u, stage, dev(yl, to, core, g))
        pltpu.make_async_copy(src.at[z], dst.at[z], rsem.at[u, stage]).start()

    def wait_all(ref, sem):
        pltpu.make_async_copy(ref, ref, sem).wait()

    ztok[...] = jnp.zeros_like(ztok)
    loads[0].wait()
    for r in range(ROWS):
        ztok[pl.ds(r * MS, COLS), :] = pair_ref[r].astype(F32)
    zt[...] = ztok[...].T
    for dy in range(2):
        for dc in range(2):
            for dg in range(NG):
                if dy or dc or dg:
                    greet(dev(yl if dy == 0 else 1 - yl, z, core if dc == 0 else mate, lax.rem(g + dg, NG)))
    for load in loads[1:]:
        load.wait()
    wabt[0] = wab_ref[0].T

    k, l = iota2((COLS, TOK))
    spread = mm(mask_ref[...].astype(F32).astype(BF16), one_hot(lax.rem(l, MS) == k))
    k, l = iota2((ROWS, TOK))
    keep = jnp.sum(jnp.where(l // MS == k, spread, 0.0), axis=0, keepdims=True)

    def lanes(h):
        return slice(HALF * h, HALF * h + HALF)

    def norm(h):
        zn[:, lanes(h)] = normalize(zt[:, lanes(h)], (0,)).astype(BF16)

    def project(u, h, e):
        base = 0 if u != e else 2 * CH
        p = mm(wabt[u, base : base + 2 * CH, :], zn[:, lanes(h)])
        value = sigmoid(p[:CH]) * p[CH:] * keep[:, lanes(h)]
        sides[e, :, NG * h : NG * h + NG, :] = value.reshape(NZ, NG, HALF)

    def push(u, e):
        s1[u, e] = sides[e].astype(BF16)
        send_z(s1.at[u, e], r1.at[u, e], u, F1 + e)

    def constants():
        wgt[0], wgt[1] = wg_ref[0].T, wg_ref[1].T
        wot[0], wot[1] = wo_ref[0].T, wo_ref[1].T
        wabt[1] = wab_ref[1].T
        o, i = iota2((256, 256))
        perm[...] = one_hot(i == lax.rem(o, 16) * 16 + o // 16)
        i, l = iota2((224, 256))
        zi, n = lax.rem(i, NZ), i // NZ
        ci = jnp.where(n < 8, n // 4, (n - 8) // 3)
        ri = jnp.where(n < 8, lax.rem(n, 4), 4 + lax.rem(n - 8, 3))
        cols[...] = one_hot(l == zi // 4 * MS + lax.rem(zi, 4) * 14 + ci * 7 + ri)

    def channels_apart(u, e):
        x = mm(perm[...], r1[u, e].reshape(256, HALF)).astype(BF16)
        for h in range(2):
            s2[u, e, :, :, lanes(h)] = x[128 * h : 128 * h + 128].reshape(NG, NZ, HALF)

    def send_early(u, a, slot):
        for d in (4, 3, 5, 2, 6, 1, 7, 0):
            h = lax.rem(g + d, NG)
            for yl_to in (yl, 1 - yl):
                send(
                    s2.at[u, EARLY, h], r2.at[u, EARLY, slot], u, F2 + EARLY, dev(yl_to, z, a, h),
                    a == core if d == 0 and yl_to is yl else None,
                )

    def send_late(u, a, slot):
        for d in (4, 3, 5, 2, 6, 1, 7, 0):
            h = lax.rem(g + d, NG)
            send(
                s2.at[u, LATE, h], r2.at[u, LATE, slot], u, F2 + LATE, dev(a, z, core, h), a == yl if d == 0 else None
            )

    def assemble(u, e, cs):
        n_src, n_g = (1, 8) if u == 0 else (2, 4)
        for s in range(n_src):
            for q in range(n_g // 2):
                for t in range(4):
                    at = slice(128 * t, 128 * t + 128)
                    slot = cs * NG + s * n_g + 2 * q
                    lo, hi = swap_halves(r2[u, e, slot, :, at], r2[u, e, slot + 1, :, at])
                    to_lanes = slice(128 * q, 128 * q + 128)
                    for r, x in ((2 * t, lo), (2 * t + 1, hi)):
                        if r == ROWS:
                            continue
                        if u == 1:
                            block = (cs * 2 + s) * ROWS + r
                        elif r < 4:
                            block = cs * 4 + r
                        else:
                            block = 8 + cs * 3 + r - 4
                        to_rows = pl.ds(pl.multiple_of(block * NZ, NZ), NZ) if cs is core or cs is mate else pl.ds(block * NZ, NZ)
                        if u == 0:
                            y0[e, to_rows, to_lanes] = x
                        else:
                            y1[e, to_rows, to_lanes] = x

    def finish(u, h):
        x = r4[u, h].astype(F32).reshape(NZ, 2, NG, 128)
        tn = jnp.concatenate([normalize(x[:, t], (0, 1)).reshape(CH, 128) for t in range(2)], axis=1).astype(BF16)
        out = mm(wot[u], tn)
        zt[:, lanes(h)] = (zt[:, lanes(h)] + gate[:, lanes(h)] * out).astype(BF16).astype(F32)

    for u in range(2):
        a = yl if u == 0 else g // 4
        slot = core * NG + g if u == 0 else (core * 2 + yl) * 4 + lax.rem(g, 4)
        if u == 0:
            norm(0)
            norm(1)
            project(u, 0, EARLY)
            project(u, 1, EARLY)
            pl.semaphore_wait(barrier, NZ - 1 + 4 * NG - 1)
            push(u, EARLY)
            project(u, 0, LATE)
            project(u, 1, LATE)
            push(u, LATE)
            constants()
        else:
            project(u, 1, EARLY)
            push(u, EARLY)
            project(u, 1, LATE)
            push(u, LATE)
        gate[...] = sigmoid(mm(wgt[u], zn[...]))

        wait_all(r1.at[u, EARLY], rsem.at[u, F1 + EARLY])
        channels_apart(u, EARLY)
        send_early(u, a, slot)
        wait_all(r1.at[u, LATE], rsem.at[u, F1 + LATE])
        channels_apart(u, LATE)
        send_late(u, a, slot)

        wait_all(r2.at[u, EARLY], rsem.at[u, F2 + EARLY])
        assemble(u, EARLY, 0)
        assemble(u, EARLY, 1)
        if u == 0:
            e0[...] = mm(y0[EARLY], cols[...], 0, 0).astype(BF16)
        else:
            e1[...] = mm(cols[...], y1[EARLY], 1, 1).astype(BF16)

        own = r2.at[u, LATE, pl.ds(core * NG, NG)]
        wait_all(own, rsem.at[u, F2 + LATE])
        hand = pltpu.make_async_remote_copy(
            src_ref=own, dst_ref=own, send_sem=ssem.at[u, MATE], recv_sem=rsem.at[u, MATE],
            device_id=dev(yl, z, mate, g), device_id_type=MESH,
        )
        hand.start()
        assemble(u, LATE, core)
        hand.wait_recv()
        assemble(u, LATE, mate)

        i_half, j_half = (yl, core) if u == 0 else (core, yl)
        for h in range(2):
            n_r = 4 - h
            rows = slice(128 * h, 128 * h + 32 * n_r)
            if u == 0:
                tri = mm(y0[LATE, rows, :], e0[...]).astype(BF16)
            else:
                tri = mm(e1[rows, :], y1[LATE]).astype(BF16)
            for ci in range(2):
                for t in range(2):
                    for q in range(2):
                        at = slice(128 * q, 128 * q + 128)
                        base = (ci * n_r + 2 * t) * NZ
                        c0 = tri[base : base + NZ, at]
                        c1 = tri[base + NZ : base + 2 * NZ, at] if 2 * t + 1 < n_r else jnp.zeros_like(c0)
                        lo, hi = swap_halves(c0, c1)
                        s3[u, h, ci * 4 + 2 * q, :, 128 * t : 128 * t + 128] = lo
                        s3[u, h, ci * 4 + 2 * q + 1, :, 128 * t : 128 * t + 128] = hi

            for d in (2, 1, 3, 0):
                q = lax.rem(g + d, 4)
                to = 4 * j_half + q
                for ci in (mate, core):
                    send(
                        s3.at[u, h, ci * 4 + q], r3.at[u, h, g], u, B1 + h, dev(i_half, z, ci, to),
                        (i_half == yl) & (to == g) if d == 0 and ci is core else None,
                    )

        for h in range(2):
            wait_all(r3.at[u, h], rsem.at[u, B1 + h])
            x = r3[u, h].reshape(NG * NZ, HALF)
            x = jnp.concatenate([x[:, :128], x[:, 128:]], axis=0)
            s4[u, h] = mm(perm[...], x).astype(BF16).reshape(NZ, 16, 128)
            send_z(s4.at[u, h], r4.at[u, h], u, B2 + h)
        for h in range(2):
            wait_all(r4.at[u, h], rsem.at[u, B2 + h])
            finish(u, h)
            if u == 0:
                norm(h)
                if h == 0:
                    project(1, h, EARLY)
                    project(1, h, LATE)

    ztok[...] = zt[...].T
    for r in range(ROWS):
        out_ref[r] = ztok[pl.ds(r * MS, COLS), :].astype(BF16)

    def wait_sent(u, stage, ref, count, less):
        @pl.when(less)
        def _():
            wait_all(ref.at[pl.ds(0, count - 1)], ssem.at[u, stage])

        @pl.when(jnp.logical_not(less))
        def _():
            wait_all(ref.at[pl.ds(0, count)], ssem.at[u, stage])

    for u in range(2):
        a = yl if u == 0 else g // 4
        for e in (EARLY, LATE):
            wait_all(s1.at[u, e, pl.ds(0, NZ - 1)], ssem.at[u, F1 + e])
        wait_sent(u, F2 + EARLY, r2.at[u, EARLY], 2 * NG, a == core)
        wait_sent(u, F2 + LATE, s2.at[u, LATE], NG, a == yl)
        wait_all(r2.at[u, LATE, pl.ds(0, NG)], ssem.at[u, MATE])
        for h in range(2):
            wait_sent(u, B1 + h, s3.at[u, h], 8, g // 4 == core if u == 0 else (core == yl) & (g // 4 == yl))
            wait_all(s4.at[u, h, pl.ds(0, NZ - 1)], ssem.at[u, B2 + h])


def body(pair, pair_mask, w_ab, w_gate, w_out):
    return pl.pallas_call(
        kernel,
        out_shape=pltpu.VMEM(pair.shape, pair.dtype),
        in_specs=[pl.BlockSpec(memory_space=pltpu.HBM)] * 5,
        out_specs=pl.BlockSpec(memory_space=pltpu.VMEM),
        scratch_shapes=[
            pltpu.VMEM((ROWS, COLS, CH), BF16),
            pltpu.VMEM((ROWS, COLS), jnp.int32),
            pltpu.VMEM((2, CH, 4 * CH), BF16),
            pltpu.VMEM((2, CH, CH), BF16),
            pltpu.VMEM((2, CH, CH), BF16),
            pltpu.VMEM((2, 4 * CH, CH), BF16),
            pltpu.VMEM((2, CH, CH), BF16),
            pltpu.VMEM((2, CH, CH), BF16),
            pltpu.VMEM((256, 256), BF16),
            pltpu.VMEM((224, 256), BF16),
            pltpu.VMEM((TOK, CH), F32),
            pltpu.VMEM((CH, TOK), F32),
            pltpu.VMEM((CH, TOK), BF16),
            pltpu.VMEM((CH, TOK), F32),
            pltpu.VMEM((2, NZ, 16, HALF), F32),
            pltpu.VMEM((2, 2, NZ, 16, HALF), BF16),
            pltpu.VMEM((2, 2, NZ, 16, HALF), BF16),
            pltpu.VMEM((2, 2, NG, NZ, TOK), BF16),
            pltpu.VMEM((2, 2, 16, NZ, TOK), BF16),
            pltpu.VMEM((2, 224, 512), BF16),
            pltpu.VMEM((2, 448, 256), BF16),
            pltpu.VMEM((512, 256), BF16),
            pltpu.VMEM((224, 448), BF16),
            pltpu.VMEM((2, 2, 8, NZ, HALF), BF16),
            pltpu.VMEM((2, 2, 8, NZ, HALF), BF16),
            pltpu.VMEM((2, 2, NZ, 16, 128), BF16),
            pltpu.VMEM((2, 2, NZ, 16, 128), BF16),
            pltpu.SemaphoreType.DMA((5,)),
            pltpu.SemaphoreType.DMA((2, STAGES)),
            pltpu.SemaphoreType.DMA((2, STAGES)),
        ],
        compiler_params=pltpu.CompilerParams(
            collective_id=0, has_side_effects=True, vmem_limit_bytes=32 * 1024 * 1024
        ),
        name="triangle",
    )(*(pltpu.with_memory_space_constraint(x, pltpu.HBM) for x in (pair, pair_mask, w_ab, w_gate, w_out)))


def solution(mesh):
    return jax.shard_map(
        body,
        mesh=mesh,
        in_specs=(P("row", "grp", None), P("row", "grp"), P(), P(), P()),
        out_specs=P("row", "grp", None),
        check_vma=False,
    )
```

time: 363 us -> 89.3 us (0.25); the launches traced: 357 us -> 89.2 us
  waiting for transfers between devices: 206 us -> 0 us
  Pallas kernels: 0 us -> 88.5 us
  blocking collectives: 69.1 us -> 0 us
  matrix products: 25 us -> 0 us
  local copies, waits for them, and re-layouts: 23.3 us -> 0.64 us
  starting transfers between devices: 16.1 us -> 0 us
  between operations: 14.1 us -> 0.01 us
  other arithmetic: 3.72 us -> 0 us
    all_gather x2 -> x0, waiting for transfers between devices: 197 us -> none  [body(): lax.all_gather(right, 'row', axis=1, tiled=True)]
    pallas_call x0 -> x1, Pallas kernels: none -> 88.5 us  [body(): pl.pallas_call(kernel, out_shape=pltpu.VMEM(pair.shape, pair.dtype), in_s...]
    all_to_all x5 -> x0, blocking collectives: 69.1 us -> none  [the longest x1 25.3 us: body(): lax.all_to_all(left, 'row', split_axis=2, concat_axis=1, tiled=True)]
    dot_general x8 -> x0, matrix products: 25 us -> none  [the longest x1 10.8 us: body(): jnp.einsum('cik,cjk->cij', left, lax.all_gather(right, 'row', axis=1, til...]
    all_to_all x2 -> x0, starting transfers between devices: 15.6 us -> none  [body(): sums = lax.all_to_all(sums, 'grp', split_axis=2, concat_axis=0, tiled=True)]
    all_to_all x11 -> x0, local copies, waits for them, and re-layouts: 11.5 us -> none  [the longest x2 7.4 us: body(): lax.all_to_all(left, 'row', split_axis=2, concat_axis=1, tiled=True)]
    all_to_all x2 -> x0, waiting for transfers between devices: 8.79 us -> none  [body(): sums = lax.all_to_all(sums, 'grp', split_axis=2, concat_axis=0, tiled=True)]
    unnamed x22 -> x1, local copies, waits for them, and re-layouts: 9.4 us -> 0.64 us
  transfers between devices with their start and end apart: 4 -> 0, of which waited for: 4 -> 0; matrix products, arithmetic and copies ran while one was open for 4% -> 0% of each run, Pallas kernels for 0% -> 0%
where the time goes in v1:
time: 89.3 us; the launch traced here: 89.2 us
  Pallas kernels  88.5 us (99%)
    pallas_call x1, Pallas kernels, body(): pl.pallas_call(kernel, out_shape=pltpu.VMEM(pair.shape, pair.dtype), in_s...  88.5 us

profile of v1, /device:TPU:24, one launch (start us, length us, event | category | flops | bytes accessed | tf_op | source)
XLA Modules:
  0.0 89.2 jit_solution(8385235813211676597)
XLA Ops:
  0.0 88.5 %triangle.1 = bf16[7,56,128]{2,1,0:T(8,128)(2,1)S(1)} custom-call(bf16[7,56,128]{2,1,0:T(8,128)(2,1)} %pair_hbm.1, s32[7,56]{1,0:T(8,128)} %mask_hbm.1, bf16[2,128,512]{2,1,0:T(8,128)(2,1)} %wab_hbm.1, bf16[2,128,128]{2,1,0:T(8,128)(2,1)} %wg_hbm.1, bf16[2,128,128]{2,1,0:T(8,128)(2,1)} %wo_hbm.1), custom_call_target="tpu_custom_call" | custom-call | tf_op jit(solution)/shard_map/triangle/pallas_call | solution.py:321
  88.5 0.6 copy.7

commit v2 on v1

--- a/solution.py
+++ b/solution.py
@@ -12,7 +12,7 @@
 HALF = TOK // 2
 AROUND = (8, 7, 9, 6, 10, 5, 11, 4, 12, 3, 13, 2, 14, 1, 15)
 EARLY, LATE = 0, 1
-F1, F2, MATE, B1, B2, STAGES = 0, 2, 4, 5, 7, 9
+F1, F2, MATE, B1, B2, STAGES = 0, 1, 3, 4, 5, 6
 
 
 def mm(a, b, ca=1, cb=0):
@@ -135,9 +135,9 @@
         value = sigmoid(p[:CH]) * p[CH:] * keep[:, lanes(h)]
         sides[e, :, NG * h : NG * h + NG, :] = value.reshape(NZ, NG, HALF)
 
-    def push(u, e):
-        s1[u, e] = sides[e].astype(BF16)
-        send_z(s1.at[u, e], r1.at[u, e], u, F1 + e)
+    def push(u):
+        s1[u] = jnp.concatenate([sides[EARLY], sides[LATE]], axis=1).astype(BF16)
+        send_z(s1.at[u], r1.at[u], u, F1)
 
     def constants():
         wgt[0], wgt[1] = wg_ref[0].T, wg_ref[1].T
@@ -152,7 +152,7 @@
         cols[...] = one_hot(l == zi // 4 * MS + lax.rem(zi, 4) * 14 + ci * 7 + ri)
 
     def channels_apart(u, e):
-        x = mm(perm[...], r1[u, e].reshape(256, HALF)).astype(BF16)
+        x = mm(perm[...], r1[u, :, 16 * e : 16 * e + 16, :].reshape(256, HALF)).astype(BF16)
         for h in range(2):
             s2[u, e, :, :, lanes(h)] = x[128 * h : 128 * h + 128].reshape(NG, NZ, HALF)
 
@@ -197,7 +197,7 @@
                             y1[e, to_rows, to_lanes] = x
 
     def finish(u, h):
-        x = r4[u, h].astype(F32).reshape(NZ, 2, NG, 128)
+        x = r4[u, :, 16 * h : 16 * h + 16, :].astype(F32).reshape(NZ, 2, NG, 128)
         tn = jnp.concatenate([normalize(x[:, t], (0, 1)).reshape(CH, 128) for t in range(2)], axis=1).astype(BF16)
         out = mm(wot[u], tn)
         zt[:, lanes(h)] = (zt[:, lanes(h)] + gate[:, lanes(h)] * out).astype(BF16).astype(F32)
@@ -208,25 +208,19 @@
         if u == 0:
             norm(0)
             norm(1)
-            project(u, 0, EARLY)
-            project(u, 1, EARLY)
+        for h in range(2):
+            project(u, h, EARLY)
+            project(u, h, LATE)
+        if u == 0:
             pl.semaphore_wait(barrier, NZ - 1 + 4 * NG - 1)
-            push(u, EARLY)
-            project(u, 0, LATE)
-            project(u, 1, LATE)
-            push(u, LATE)
+        push(u)
+        if u == 0:
             constants()
-        else:
-            project(u, 1, EARLY)
-            push(u, EARLY)
-            project(u, 1, LATE)
-            push(u, LATE)
         gate[...] = sigmoid(mm(wgt[u], zn[...]))
 
-        wait_all(r1.at[u, EARLY], rsem.at[u, F1 + EARLY])
+        wait_all(r1.at[u], rsem.at[u, F1])
         channels_apart(u, EARLY)
         send_early(u, a, slot)
-        wait_all(r1.at[u, LATE], rsem.at[u, F1 + LATE])
         channels_apart(u, LATE)
         send_late(u, a, slot)
 
@@ -265,32 +259,36 @@
                         c0 = tri[base : base + NZ, at]
                         c1 = tri[base + NZ : base + 2 * NZ, at] if 2 * t + 1 < n_r else jnp.zeros_like(c0)
                         lo, hi = swap_halves(c0, c1)
-                        s3[u, h, ci * 4 + 2 * q, :, 128 * t : 128 * t + 128] = lo
-                        s3[u, h, ci * 4 + 2 * q + 1, :, 128 * t : 128 * t + 128] = hi
-
-            for d in (2, 1, 3, 0):
-                q = lax.rem(g + d, 4)
-                to = 4 * j_half + q
-                for ci in (mate, core):
-                    send(
-                        s3.at[u, h, ci * 4 + q], r3.at[u, h, g], u, B1 + h, dev(i_half, z, ci, to),
-                        (i_half == yl) & (to == g) if d == 0 and ci is core else None,
-                    )
-
+                        tile = slice(HALF * h + 128 * t, HALF * h + 128 * t + 128)
+                        s3[u, ci * 4 + 2 * q, :, tile] = lo
+                        s3[u, ci * 4 + 2 * q + 1, :, tile] = hi
+
+        for d in (2, 1, 3, 0):
+            q = lax.rem(g + d, 4)
+            to = 4 * j_half + q
+            for ci in (mate, core):
+                send(
+                    s3.at[u, ci * 4 + q], r3.at[u, g], u, B1, dev(i_half, z, ci, to),
+                    (i_half == yl) & (to == g) if d == 0 and ci is core else None,
+                )
+
+        wait_all(r3.at[u], rsem.at[u, B1])
+        x = r3[u].reshape(NG * NZ, TOK)
+        x = jnp.concatenate(
+            [
+                jnp.concatenate([x[:, :128], x[:, 256:384]], axis=1),
+                jnp.concatenate([x[:, 128:256], x[:, 384:]], axis=1),
+            ],
+            axis=0,
+        )
+        x = mm(perm[...], x).astype(BF16).reshape(NZ, 16, 256)
+        s4[u] = jnp.concatenate([x[:, :, :128], x[:, :, 128:]], axis=1)
+        send_z(s4.at[u], r4.at[u], u, B2)
+        wait_all(r4.at[u], rsem.at[u, B2])
         for h in range(2):
-            wait_all(r3.at[u, h], rsem.at[u, B1 + h])
-            x = r3[u, h].reshape(NG * NZ, HALF)
-            x = jnp.concatenate([x[:, :128], x[:, 128:]], axis=0)
-            s4[u, h] = mm(perm[...], x).astype(BF16).reshape(NZ, 16, 128)
-            send_z(s4.at[u, h], r4.at[u, h], u, B2 + h)
-        for h in range(2):
-            wait_all(r4.at[u, h], rsem.at[u, B2 + h])
             finish(u, h)
             if u == 0:
                 norm(h)
-                if h == 0:
-                    project(1, h, EARLY)
-                    project(1, h, LATE)
 
     ztok[...] = zt[...].T
     for r in range(ROWS):
@@ -307,14 +305,12 @@
 
     for u in range(2):
         a = yl if u == 0 else g // 4
-        for e in (EARLY, LATE):
-            wait_all(s1.at[u, e, pl.ds(0, NZ - 1)], ssem.at[u, F1 + e])
+        wait_all(s1.at[u, pl.ds(0, NZ - 1)], ssem.at[u, F1])
         wait_sent(u, F2 + EARLY, r2.at[u, EARLY], 2 * NG, a == core)
         wait_sent(u, F2 + LATE, s2.at[u, LATE], NG, a == yl)
         wait_all(r2.at[u, LATE, pl.ds(0, NG)], ssem.at[u, MATE])
-        for h in range(2):
-            wait_sent(u, B1 + h, s3.at[u, h], 8, g // 4 == core if u == 0 else (core == yl) & (g // 4 == yl))
-            wait_all(s4.at[u, h, pl.ds(0, NZ - 1)], ssem.at[u, B2 + h])
+        wait_sent(u, B1, s3.at[u], 8, g // 4 == core if u == 0 else (core == yl) & (g // 4 == yl))
+        wait_all(s4.at[u, pl.ds(0, NZ - 1)], ssem.at[u, B2])
 
 
 def body(pair, pair_mask, w_ab, w_gate, w_out):
@@ -339,18 +335,18 @@
             pltpu.VMEM((CH, TOK), BF16),
             pltpu.VMEM((CH, TOK), F32),
             pltpu.VMEM((2, NZ, 16, HALF), F32),
-            pltpu.VMEM((2, 2, NZ, 16, HALF), BF16),
-            pltpu.VMEM((2, 2, NZ, 16, HALF), BF16),
+            pltpu.VMEM((2, NZ, 32, HALF), BF16),
+            pltpu.VMEM((2, NZ, 32, HALF), BF16),
             pltpu.VMEM((2, 2, NG, NZ, TOK), BF16),
             pltpu.VMEM((2, 2, 16, NZ, TOK), BF16),
             pltpu.VMEM((2, 224, 512), BF16),
             pltpu.VMEM((2, 448, 256), BF16),
             pltpu.VMEM((512, 256), BF16),
             pltpu.VMEM((224, 448), BF16),
-            pltpu.VMEM((2, 2, 8, NZ, HALF), BF16),
-            pltpu.VMEM((2, 2, 8, NZ, HALF), BF16),
-            pltpu.VMEM((2, 2, NZ, 16, 128), BF16),
-            pltpu.VMEM((2, 2, NZ, 16, 128), BF16),
+            pltpu.VMEM((2, 8, NZ, TOK), BF16),
+            pltpu.VMEM((2, 8, NZ, TOK), BF16),
+            pltpu.VMEM((2, NZ, 32, 128), BF16),
+            pltpu.VMEM((2, NZ, 32, 128), BF16),
             pltpu.SemaphoreType.DMA((5,)),
             pltpu.SemaphoreType.DMA((2, STAGES)),
             pltpu.SemaphoreType.DMA((2, STAGES)),

time: 89.3 us -> 89.3 us (level)
  no operation moved by 1% of the time
where the time goes in v2:
time: 89.3 us; the launch traced here: 89.2 us
  Pallas kernels  88.5 us (99%)
    pallas_call x1, Pallas kernels, body(): pl.pallas_call(kernel, out_shape=pltpu.VMEM(pair.shape, pair.dtype), in_s...  88.5 us

profile of v2, /device:TPU:24, one launch (start us, length us, event | category | flops | bytes accessed | tf_op | source)
XLA Modules:
  0.0 89.2 jit_solution(10401330838020936751)
XLA Ops:
  0.0 88.5 %triangle.1 = bf16[7,56,128]{2,1,0:T(8,128)(2,1)S(1)} custom-call(bf16[7,56,128]{2,1,0:T(8,128)(2,1)} %pair_hbm.1, s32[7,56]{1,0:T(8,128)} %mask_hbm.1, bf16[2,128,512]{2,1,0:T(8,128)(2,1)} %wab_hbm.1, bf16[2,128,128]{2,1,0:T(8,128)(2,1)} %wg_hbm.1, bf16[2,128,128]{2,1,0:T(8,128)(2,1)} %wo_hbm.1), custom_call_target="tpu_custom_call" | custom-call | tf_op jit(solution)/shard_map/triangle/pallas_call | solution.py:317
  88.5 0.6 copy.7

commit v3 on v1

--- a/solution.py
+++ b/solution.py
@@ -11,8 +11,9 @@
 TOK = RS * MS
 HALF = TOK // 2
 AROUND = (8, 7, 9, 6, 10, 5, 11, 4, 12, 3, 13, 2, 14, 1, 15)
+FAR = (6, 5, 7, 2, 4, 1, 3, 0)
 EARLY, LATE = 0, 1
-F1, F2, MATE, B1, B2, STAGES = 0, 2, 4, 5, 7, 9
+F1, F2, B1, B2, STAGES = 0, 2, 4, 6, 8
 
 
 def mm(a, b, ca=1, cb=0):
@@ -41,20 +42,18 @@
     return 0.5 * jnp.tanh(0.5 * x) + 0.5
 
 
-def swap_halves(a, b):
-    low = lax.broadcasted_iota(jnp.int32, a.shape, a.ndim - 1) < 64
-    return jnp.where(low, a, pltpu.roll(b, 64, a.ndim - 1)), jnp.where(low, pltpu.roll(a, 64, a.ndim - 1), b)
-
-
 def kernel(
     pair_hbm, mask_hbm, wab_hbm, wg_hbm, wo_hbm, out_ref,
     pair_ref, mask_ref, wab_ref, wg_ref, wo_ref, wabt, wgt, wot, perm, cols,
-    ztok, zt, zn, gate, sides, s1, r1, s2, r2, y0, y1, e0, e1, s3, r3, s4, r4, insem, ssem, rsem,
+    ztok, zt, zn, gate, s1, r1, s2, r2, y0, y1, e0, e1, s3, r3, s4, r4, insem, ssem, rsem,
 ):
     loads = [
         pltpu.make_async_copy(src, dst, insem.at[n])
         for n, (src, dst) in enumerate(
-            ((pair_hbm, pair_ref), (wab_hbm, wab_ref), (mask_hbm, mask_ref), (wg_hbm, wg_ref), (wo_hbm, wo_ref))
+            (
+                (pair_hbm, pair_ref), (wab_hbm.at[0], wab_ref.at[0]), (mask_hbm, mask_ref), (wab_hbm.at[1], wab_ref.at[1]),
+                (wg_hbm, wg_ref), (wo_hbm, wo_ref),
+            )
         )
     ]
     for load in loads:
@@ -66,6 +65,7 @@
     yl = row // (2 * NZ)
 
     mate = 1 - core
+    odd = lax.rem(g, 2)
 
     def dev(yl_, z_, core_, g_):
         return (yl_ * (2 * NZ) + z_ * 2 + core_, g_)
@@ -77,6 +77,11 @@
 
     for d in AROUND:
         greet(dev(yl, lax.rem(z + d, NZ), core, g))
+    for d in FAR:
+        for yl_to in (yl, 1 - yl):
+            for core_to in (core, mate):
+                if d or yl_to is not yl or core_to is not core:
+                    greet(dev(yl_to, z, core_to, lax.rem(g + d, NG)))
 
     def send(src, dst, u, stage, device, is_self=None):
         def remote():
@@ -104,24 +109,25 @@
     def wait_all(ref, sem):
         pltpu.make_async_copy(ref, ref, sem).wait()
 
+    def slot_rows(r):
+        return pl.ds(pl.multiple_of((r + odd * (1 - 2 * (r % 2))) * MS, MS), COLS)
+
+    low = lax.broadcasted_iota(jnp.int32, (NZ, 128), 1) < 64
     ztok[...] = jnp.zeros_like(ztok)
+
+    k, l = iota2((COLS, TOK))
+    places = one_hot(lax.rem(l, MS) == k)
+    k, l = iota2((ROWS, TOK))
+    loads[2].wait()
+    spread = mm(mask_ref[...].astype(F32).astype(BF16), places)
+    keep = jnp.sum(jnp.where(l // MS == k + odd * (1 - 2 * lax.rem(k, 2)), spread, 0.0), axis=0, keepdims=True)
+
+    loads[1].wait()
+    wabt[0] = wab_ref[0].T
     loads[0].wait()
     for r in range(ROWS):
-        ztok[pl.ds(r * MS, COLS), :] = pair_ref[r].astype(F32)
+        ztok[slot_rows(r), :] = pair_ref[r].astype(F32)
     zt[...] = ztok[...].T
-    for dy in range(2):
-        for dc in range(2):
-            for dg in range(NG):
-                if dy or dc or dg:
-                    greet(dev(yl if dy == 0 else 1 - yl, z, core if dc == 0 else mate, lax.rem(g + dg, NG)))
-    for load in loads[1:]:
-        load.wait()
-    wabt[0] = wab_ref[0].T
-
-    k, l = iota2((COLS, TOK))
-    spread = mm(mask_ref[...].astype(F32).astype(BF16), one_hot(lax.rem(l, MS) == k))
-    k, l = iota2((ROWS, TOK))
-    keep = jnp.sum(jnp.where(l // MS == k, spread, 0.0), axis=0, keepdims=True)
 
     def lanes(h):
         return slice(HALF * h, HALF * h + HALF)
@@ -129,17 +135,18 @@
     def norm(h):
         zn[:, lanes(h)] = normalize(zt[:, lanes(h)], (0,)).astype(BF16)
 
-    def project(u, h, e):
-        base = 0 if u != e else 2 * CH
-        p = mm(wabt[u, base : base + 2 * CH, :], zn[:, lanes(h)])
-        value = sigmoid(p[:CH]) * p[CH:] * keep[:, lanes(h)]
-        sides[e, :, NG * h : NG * h + NG, :] = value.reshape(NZ, NG, HALF)
-
-    def push(u, e):
-        s1[u, e] = sides[e].astype(BF16)
-        send_z(s1.at[u, e], r1.at[u, e], u, F1 + e)
+    def push(u, h):
+        def side(base):
+            p = mm(wabt[u, base : base + 2 * CH, :], zn[:, lanes(h)])
+            return (sigmoid(p[:CH]) * p[CH:] * keep[:, lanes(h)]).reshape(NZ, NG, HALF)
+
+        left, right = side(0), side(2 * CH)
+        s1[u, h] = jnp.concatenate([right, left] if u == 0 else [left, right], axis=1).astype(BF16)
+        send_z(s1.at[u, h], r1.at[u, h], u, F1 + h)
 
     def constants():
+        for load in loads[3:]:
+            load.wait()
         wgt[0], wgt[1] = wg_ref[0].T, wg_ref[1].T
         wot[0], wot[1] = wo_ref[0].T, wo_ref[1].T
         wabt[1] = wab_ref[1].T
@@ -151,13 +158,13 @@
         ri = jnp.where(n < 8, lax.rem(n, 4), 4 + lax.rem(n - 8, 3))
         cols[...] = one_hot(l == zi // 4 * MS + lax.rem(zi, 4) * 14 + ci * 7 + ri)
 
-    def channels_apart(u, e):
-        x = mm(perm[...], r1[u, e].reshape(256, HALF)).astype(BF16)
-        for h in range(2):
-            s2[u, e, :, :, lanes(h)] = x[128 * h : 128 * h + 128].reshape(NG, NZ, HALF)
+    def channels_apart(u, h):
+        x = mm(perm[...], r1[u, h].reshape(256, HALF)).astype(BF16)
+        for e in (EARLY, LATE):
+            s2[u, e, :, :, lanes(h)] = x[128 * e : 128 * e + 128].reshape(NG, NZ, HALF)
 
     def send_early(u, a, slot):
-        for d in (4, 3, 5, 2, 6, 1, 7, 0):
+        for d in FAR:
             h = lax.rem(g + d, NG)
             for yl_to in (yl, 1 - yl):
                 send(
@@ -166,11 +173,13 @@
                 )
 
     def send_late(u, a, slot):
-        for d in (4, 3, 5, 2, 6, 1, 7, 0):
+        for d in FAR:
             h = lax.rem(g + d, NG)
-            send(
-                s2.at[u, LATE, h], r2.at[u, LATE, slot], u, F2 + LATE, dev(a, z, core, h), a == yl if d == 0 else None
-            )
+            for core_to in (core, mate):
+                send(
+                    s2.at[u, LATE, h], r2.at[u, LATE, slot], u, F2 + LATE, dev(a, z, core_to, h),
+                    a == yl if d == 0 and core_to is core else None,
+                )
 
     def assemble(u, e, cs):
         n_src, n_g = (1, 8) if u == 0 else (2, 4)
@@ -179,7 +188,9 @@
                 for t in range(4):
                     at = slice(128 * t, 128 * t + 128)
                     slot = cs * NG + s * n_g + 2 * q
-                    lo, hi = swap_halves(r2[u, e, slot, :, at], r2[u, e, slot + 1, :, at])
+                    even, other = r2[u, e, slot, :, at], r2[u, e, slot + 1, :, at]
+                    lo = jnp.where(low, even, other)
+                    hi = pltpu.roll(jnp.where(low, other, even), 64, 1) if t < 3 else None
                     to_lanes = slice(128 * q, 128 * q + 128)
                     for r, x in ((2 * t, lo), (2 * t + 1, hi)):
                         if r == ROWS:
@@ -190,7 +201,7 @@
                             block = cs * 4 + r
                         else:
                             block = 8 + cs * 3 + r - 4
-                        to_rows = pl.ds(pl.multiple_of(block * NZ, NZ), NZ) if cs is core or cs is mate else pl.ds(block * NZ, NZ)
+                        to_rows = slice(block * NZ, block * NZ + NZ)
                         if u == 0:
                             y0[e, to_rows, to_lanes] = x
                         else:
@@ -207,27 +218,17 @@
         slot = core * NG + g if u == 0 else (core * 2 + yl) * 4 + lax.rem(g, 4)
         if u == 0:
             norm(0)
+            pl.semaphore_wait(barrier, NZ - 1 + 4 * NG - 1)
+            push(u, 0)
             norm(1)
-            project(u, 0, EARLY)
-            project(u, 1, EARLY)
-            pl.semaphore_wait(barrier, NZ - 1 + 4 * NG - 1)
-            push(u, EARLY)
-            project(u, 0, LATE)
-            project(u, 1, LATE)
-            push(u, LATE)
+            push(u, 1)
             constants()
-        else:
-            project(u, 1, EARLY)
-            push(u, EARLY)
-            project(u, 1, LATE)
-            push(u, LATE)
         gate[...] = sigmoid(mm(wgt[u], zn[...]))
 
-        wait_all(r1.at[u, EARLY], rsem.at[u, F1 + EARLY])
-        channels_apart(u, EARLY)
+        for h in range(2):
+            wait_all(r1.at[u, h], rsem.at[u, F1 + h])
+            channels_apart(u, h)
         send_early(u, a, slot)
-        wait_all(r1.at[u, LATE], rsem.at[u, F1 + LATE])
-        channels_apart(u, LATE)
         send_late(u, a, slot)
 
         wait_all(r2.at[u, EARLY], rsem.at[u, F2 + EARLY])
@@ -238,16 +239,9 @@
         else:
             e1[...] = mm(cols[...], y1[EARLY], 1, 1).astype(BF16)
 
-        own = r2.at[u, LATE, pl.ds(core * NG, NG)]
-        wait_all(own, rsem.at[u, F2 + LATE])
-        hand = pltpu.make_async_remote_copy(
-            src_ref=own, dst_ref=own, send_sem=ssem.at[u, MATE], recv_sem=rsem.at[u, MATE],
-            device_id=dev(yl, z, mate, g), device_id_type=MESH,
-        )
-        hand.start()
-        assemble(u, LATE, core)
-        hand.wait_recv()
-        assemble(u, LATE, mate)
+        wait_all(r2.at[u, LATE], rsem.at[u, F2 + LATE])
+        assemble(u, LATE, 0)
+        assemble(u, LATE, 1)
 
         i_half, j_half = (yl, core) if u == 0 else (core, yl)
         for h in range(2):
@@ -264,9 +258,9 @@
                         base = (ci * n_r + 2 * t) * NZ
                         c0 = tri[base : base + NZ, at]
                         c1 = tri[base + NZ : base + 2 * NZ, at] if 2 * t + 1 < n_r else jnp.zeros_like(c0)
-                        lo, hi = swap_halves(c0, c1)
-                        s3[u, h, ci * 4 + 2 * q, :, 128 * t : 128 * t + 128] = lo
-                        s3[u, h, ci * 4 + 2 * q + 1, :, 128 * t : 128 * t + 128] = hi
+                        c1 = pltpu.roll(c1, 64, 1)
+                        s3[u, h, ci * 4 + 2 * q, :, 128 * t : 128 * t + 128] = jnp.where(low, c0, c1)
+                        s3[u, h, ci * 4 + 2 * q + 1, :, 128 * t : 128 * t + 128] = jnp.where(low, c1, c0)
 
             for d in (2, 1, 3, 0):
                 q = lax.rem(g + d, 4)
@@ -288,13 +282,11 @@
             finish(u, h)
             if u == 0:
                 norm(h)
-                if h == 0:
-                    project(1, h, EARLY)
-                    project(1, h, LATE)
+                push(1, h)
 
     ztok[...] = zt[...].T
     for r in range(ROWS):
-        out_ref[r] = ztok[pl.ds(r * MS, COLS), :].astype(BF16)
+        out_ref[r] = ztok[slot_rows(r), :].astype(BF16)
 
     def wait_sent(u, stage, ref, count, less):
         @pl.when(less)
@@ -307,11 +299,10 @@
 
     for u in range(2):
         a = yl if u == 0 else g // 4
-        for e in (EARLY, LATE):
-            wait_all(s1.at[u, e, pl.ds(0, NZ - 1)], ssem.at[u, F1 + e])
+        for h in range(2):
+            wait_all(s1.at[u, h, pl.ds(0, NZ - 1)], ssem.at[u, F1 + h])
         wait_sent(u, F2 + EARLY, r2.at[u, EARLY], 2 * NG, a == core)
-        wait_sent(u, F2 + LATE, s2.at[u, LATE], NG, a == yl)
-        wait_all(r2.at[u, LATE, pl.ds(0, NG)], ssem.at[u, MATE])
+        wait_sent(u, F2 + LATE, r2.at[u, LATE], 2 * NG, a == yl)
         for h in range(2):
             wait_sent(u, B1 + h, s3.at[u, h], 8, g // 4 == core if u == 0 else (core == yl) & (g // 4 == yl))
             wait_all(s4.at[u, h, pl.ds(0, NZ - 1)], ssem.at[u, B2 + h])
@@ -338,7 +329,6 @@
             pltpu.VMEM((CH, TOK), F32),
             pltpu.VMEM((CH, TOK), BF16),
             pltpu.VMEM((CH, TOK), F32),
-            pltpu.VMEM((2, NZ, 16, HALF), F32),
             pltpu.VMEM((2, 2, NZ, 16, HALF), BF16),
             pltpu.VMEM((2, 2, NZ, 16, HALF), BF16),
             pltpu.VMEM((2, 2, NG, NZ, TOK), BF16),
@@ -351,7 +341,7 @@
             pltpu.VMEM((2, 2, 8, NZ, HALF), BF16),
             pltpu.VMEM((2, 2, NZ, 16, 128), BF16),
             pltpu.VMEM((2, 2, NZ, 16, 128), BF16),
-            pltpu.SemaphoreType.DMA((5,)),
+            pltpu.SemaphoreType.DMA((6,)),
             pltpu.SemaphoreType.DMA((2, STAGES)),
             pltpu.SemaphoreType.DMA((2, STAGES)),
         ],

time: 89.3 us -> 89.6 us (level)
  no operation moved by 1% of the time
where the time goes in v3:
time: 89.6 us; the launch traced here: 88.6 us
  Pallas kernels  87.9 us (98%)
    pallas_call x1, Pallas kernels, body(): pl.pallas_call(kernel, out_shape=pltpu.VMEM(pair.shape, pair.dtype), in_s...  87.9 us

profile of v3, /device:TPU:24, one launch (start us, length us, event | category | flops | bytes accessed | tf_op | source)
XLA Modules:
  0.0 88.6 jit_solution(10048950434218718701)
XLA Ops:
  0.0 87.9 %triangle.1 = bf16[7,56,128]{2,1,0:T(8,128)(2,1)S(1)} custom-call(bf16[7,56,128]{2,1,0:T(8,128)(2,1)} %pair_hbm.1, s32[7,56]{1,0:T(8,128)} %mask_hbm.1, bf16[2,128,512]{2,1,0:T(8,128)(2,1)} %wab_hbm.1, bf16[2,128,128]{2,1,0:T(8,128)(2,1)} %wg_hbm.1, bf16[2,128,128]{2,1,0:T(8,128)(2,1)} %wo_hbm.1), custom_call_target="tpu_custom_call" | custom-call | tf_op jit(solution)/shard_map/triangle/pallas_call | solution.py:312
  87.9 0.6 copy.7

commit v4 on v3

--- a/solution.py
+++ b/solution.py
@@ -13,7 +13,7 @@
 AROUND = (8, 7, 9, 6, 10, 5, 11, 4, 12, 3, 13, 2, 14, 1, 15)
 FAR = (6, 5, 7, 2, 4, 1, 3, 0)
 EARLY, LATE = 0, 1
-F1, F2, B1, B2, STAGES = 0, 2, 4, 6, 8
+F1, F2, B1, B2, STAGES = 0, 2, 6, 8, 10
 
 
 def mm(a, b, ca=1, cb=0):
@@ -161,51 +161,43 @@
     def channels_apart(u, h):
         x = mm(perm[...], r1[u, h].reshape(256, HALF)).astype(BF16)
         for e in (EARLY, LATE):
-            s2[u, e, :, :, lanes(h)] = x[128 * e : 128 * e + 128].reshape(NG, NZ, HALF)
-
-    def send_early(u, a, slot):
+            s2[u, e, h] = x[128 * e : 128 * e + 128].reshape(NG, NZ, HALF)
+
+    def send_early(u, t, a, slot):
         for d in FAR:
             h = lax.rem(g + d, NG)
             for yl_to in (yl, 1 - yl):
                 send(
-                    s2.at[u, EARLY, h], r2.at[u, EARLY, slot], u, F2 + EARLY, dev(yl_to, z, a, h),
+                    s2.at[u, EARLY, t, h], r2.at[u, EARLY, t, slot], u, F2 + t, dev(yl_to, z, a, h),
                     a == core if d == 0 and yl_to is yl else None,
                 )
 
-    def send_late(u, a, slot):
+    def send_late(u, t, a, slot):
         for d in FAR:
             h = lax.rem(g + d, NG)
             for core_to in (core, mate):
                 send(
-                    s2.at[u, LATE, h], r2.at[u, LATE, slot], u, F2 + LATE, dev(a, z, core_to, h),
+                    s2.at[u, LATE, t, h], r2.at[u, LATE, t, slot], u, F2 + 2 + t, dev(a, z, core_to, h),
                     a == yl if d == 0 and core_to is core else None,
                 )
 
-    def assemble(u, e, cs):
-        n_src, n_g = (1, 8) if u == 0 else (2, 4)
+    def assemble(u, e, h):
+        n_src, n_g = (2, 8) if u == 0 else (4, 4)
+        to = y0 if u == 0 else y1
         for s in range(n_src):
             for q in range(n_g // 2):
-                for t in range(4):
+                for t in range(2):
                     at = slice(128 * t, 128 * t + 128)
-                    slot = cs * NG + s * n_g + 2 * q
-                    even, other = r2[u, e, slot, :, at], r2[u, e, slot + 1, :, at]
-                    lo = jnp.where(low, even, other)
-                    hi = pltpu.roll(jnp.where(low, other, even), 64, 1) if t < 3 else None
+                    even, other = r2[u, e, h, s * n_g + 2 * q, :, at], r2[u, e, h, s * n_g + 2 * q + 1, :, at]
+                    r = 4 * h + 2 * t
+                    if u == 1:
+                        row = (s * ROWS + r) * NZ
+                    else:
+                        row = (s * 4 + r if h == 0 else 8 + s * 3 + r - 4) * NZ
                     to_lanes = slice(128 * q, 128 * q + 128)
-                    for r, x in ((2 * t, lo), (2 * t + 1, hi)):
-                        if r == ROWS:
-                            continue
-                        if u == 1:
-                            block = (cs * 2 + s) * ROWS + r
-                        elif r < 4:
-                            block = cs * 4 + r
-                        else:
-                            block = 8 + cs * 3 + r - 4
-                        to_rows = slice(block * NZ, block * NZ + NZ)
-                        if u == 0:
-                            y0[e, to_rows, to_lanes] = x
-                        else:
-                            y1[e, to_rows, to_lanes] = x
+                    to[e, row : row + NZ, to_lanes] = jnp.where(low, even, other)
+                    if r + 1 < ROWS:
+                        to[e, row + NZ : row + 2 * NZ, to_lanes] = pltpu.roll(jnp.where(low, other, even), 64, 1)
 
     def finish(u, h):
         x = r4[u, h].astype(F32).reshape(NZ, 2, NG, 128)
@@ -221,26 +213,28 @@
             pl.semaphore_wait(barrier, NZ - 1 + 4 * NG - 1)
             push(u, 0)
             norm(1)
-            push(u, 1)
             constants()
         gate[...] = sigmoid(mm(wgt[u], zn[...]))
+        if u == 0:
+            push(u, 1)
 
         for h in range(2):
             wait_all(r1.at[u, h], rsem.at[u, F1 + h])
             channels_apart(u, h)
-        send_early(u, a, slot)
-        send_late(u, a, slot)
-
-        wait_all(r2.at[u, EARLY], rsem.at[u, F2 + EARLY])
-        assemble(u, EARLY, 0)
+            send_early(u, h, a, slot)
+            send_late(u, h, a, slot)
+
+        for e in (EARLY, LATE):
+            wait_all(r2.at[u, e, 0], rsem.at[u, F2 + 2 * e])
+            assemble(u, e, 0)
+        wait_all(r2.at[u, EARLY, 1], rsem.at[u, F2 + 1])
         assemble(u, EARLY, 1)
         if u == 0:
             e0[...] = mm(y0[EARLY], cols[...], 0, 0).astype(BF16)
         else:
             e1[...] = mm(cols[...], y1[EARLY], 1, 1).astype(BF16)
 
-        wait_all(r2.at[u, LATE], rsem.at[u, F2 + LATE])
-        assemble(u, LATE, 0)
+        wait_all(r2.at[u, LATE, 1], rsem.at[u, F2 + 3])
         assemble(u, LATE, 1)
 
         i_half, j_half = (yl, core) if u == 0 else (core, yl)
@@ -301,9 +295,9 @@
         a = yl if u == 0 else g // 4
         for h in range(2):
             wait_all(s1.at[u, h, pl.ds(0, NZ - 1)], ssem.at[u, F1 + h])
-        wait_sent(u, F2 + EARLY, r2.at[u, EARLY], 2 * NG, a == core)
-        wait_sent(u, F2 + LATE, r2.at[u, LATE], 2 * NG, a == yl)
-        for h in range(2):
+        for h in range(2):
+            wait_sent(u, F2 + h, r2.at[u, EARLY, h], 2 * NG, a == core)
+            wait_sent(u, F2 + 2 + h, r2.at[u, LATE, h], 2 * NG, a == yl)
             wait_sent(u, B1 + h, s3.at[u, h], 8, g // 4 == core if u == 0 else (core == yl) & (g // 4 == yl))
             wait_all(s4.at[u, h, pl.ds(0, NZ - 1)], ssem.at[u, B2 + h])
 
@@ -331,8 +325,8 @@
             pltpu.VMEM((CH, TOK), F32),
             pltpu.VMEM((2, 2, NZ, 16, HALF), BF16),
             pltpu.VMEM((2, 2, NZ, 16, HALF), BF16),
-            pltpu.VMEM((2, 2, NG, NZ, TOK), BF16),
-            pltpu.VMEM((2, 2, 16, NZ, TOK), BF16),
+            pltpu.VMEM((2, 2, 2, NG, NZ, HALF), BF16),
+            pltpu.VMEM((2, 2, 2, 16, NZ, HALF), BF16),
             pltpu.VMEM((2, 224, 512), BF16),
             pltpu.VMEM((2, 448, 256), BF16),
             pltpu.VMEM((512, 256), BF16),

time: 89.6 us -> 86 us (0.960)
  Pallas kernels: 87.9 us -> 83.8 us
    pallas_call x1, Pallas kernels: 87.9 us -> 83.8 us  [body(): pl.pallas_call(kernel, out_shape=pltpu.VMEM(pair.shape, pair.dtype), in_s...]
where the time goes in v4:
time: 86 us; the launch traced here: 84.5 us
  Pallas kernels  83.8 us (97%)
    pallas_call x1, Pallas kernels, body(): pl.pallas_call(kernel, out_shape=pltpu.VMEM(pair.shape, pair.dtype), in_s...  83.8 us

profile of v4, /device:TPU:24, one launch (start us, length us, event | category | flops | bytes accessed | tf_op | source)
XLA Modules:
  0.0 84.5 jit_solution(12922765370505138861)
XLA Ops:
  0.0 83.8 %triangle.1 = bf16[7,56,128]{2,1,0:T(8,128)(2,1)S(1)} custom-call(bf16[7,56,128]{2,1,0:T(8,128)(2,1)} %pair_hbm.1, s32[7,56]{1,0:T(8,128)} %mask_hbm.1, bf16[2,128,512]{2,1,0:T(8,128)(2,1)} %wab_hbm.1, bf16[2,128,128]{2,1,0:T(8,128)(2,1)} %wg_hbm.1, bf16[2,128,128]{2,1,0:T(8,128)(2,1)} %wo_hbm.1), custom_call_target="tpu_custom_call" | custom-call | tf_op jit(solution)/shard_map/triangle/pallas_call | solution.py:306
  83.8 0.6 copy.7

commit v5 on v4

--- a/solution.py
+++ b/solution.py
@@ -13,7 +13,8 @@
 AROUND = (8, 7, 9, 6, 10, 5, 11, 4, 12, 3, 13, 2, 14, 1, 15)
 FAR = (6, 5, 7, 2, 4, 1, 3, 0)
 EARLY, LATE = 0, 1
-F1, F2, B1, B2, STAGES = 0, 2, 6, 8, 10
+PIECES = ((0, 2), (2, 1), (3, 1))
+F1, F2, B1, B2, STAGES = 0, 3, 9, 11, 13
 
 
 def mm(a, b, ca=1, cb=0):
@@ -45,7 +46,7 @@
 def kernel(
     pair_hbm, mask_hbm, wab_hbm, wg_hbm, wo_hbm, out_ref,
     pair_ref, mask_ref, wab_ref, wg_ref, wo_ref, wabt, wgt, wot, perm, cols,
-    ztok, zt, zn, gate, s1, r1, s2, r2, y0, y1, e0, e1, s3, r3, s4, r4, insem, ssem, rsem,
+    ztok, zt, zn, gate, s1a, s1b, s1c, r1a, r1b, r1c, s2a, s2b, s2c, r2a, r2b, r2c, y0, y1, e0, e1, s3, r3, s4, r4, insem, ssem, rsem,
 ):
     loads = [
         pltpu.make_async_copy(src, dst, insem.at[n])
@@ -72,6 +73,8 @@
 
     barrier = pltpu.get_barrier_semaphore()
 
+    s1, r1, s2, r2 = (s1a, s1b, s1c), (r1a, r1b, r1c), (s2a, s2b, s2c), (r2a, r2b, r2c)
+
     def greet(device):
         pl.semaphore_signal(barrier, inc=1, device_id=device, device_id_type=MESH)
 
@@ -141,8 +144,11 @@
             return (sigmoid(p[:CH]) * p[CH:] * keep[:, lanes(h)]).reshape(NZ, NG, HALF)
 
         left, right = side(0), side(2 * CH)
-        s1[u, h] = jnp.concatenate([right, left] if u == 0 else [left, right], axis=1).astype(BF16)
-        send_z(s1.at[u, h], r1.at[u, h], u, F1 + h)
+        x = jnp.concatenate([right, left] if u == 0 else [left, right], axis=1).astype(BF16)
+        for p, (t, n) in enumerate(PIECES):
+            if t // 2 == h:
+                s1[p][u] = x[:, :, 128 * (t - 2 * h) : 128 * (t - 2 * h + n)]
+                send_z(s1[p].at[u], r1[p].at[u], u, F1 + p)
 
     def constants():
         for load in loads[3:]:
@@ -158,42 +164,43 @@
         ri = jnp.where(n < 8, lax.rem(n, 4), 4 + lax.rem(n - 8, 3))
         cols[...] = one_hot(l == zi // 4 * MS + lax.rem(zi, 4) * 14 + ci * 7 + ri)
 
-    def channels_apart(u, h):
-        x = mm(perm[...], r1[u, h].reshape(256, HALF)).astype(BF16)
+    def channels_apart(u, p):
+        width = 128 * PIECES[p][1]
+        x = mm(perm[...], r1[p][u].reshape(256, width)).astype(BF16)
         for e in (EARLY, LATE):
-            s2[u, e, h] = x[128 * e : 128 * e + 128].reshape(NG, NZ, HALF)
-
-    def send_early(u, t, a, slot):
+            s2[p][u, e] = x[128 * e : 128 * e + 128].reshape(NG, NZ, width)
+
+    def send_early(u, p, a, slot):
         for d in FAR:
             h = lax.rem(g + d, NG)
             for yl_to in (yl, 1 - yl):
                 send(
-                    s2.at[u, EARLY, t, h], r2.at[u, EARLY, t, slot], u, F2 + t, dev(yl_to, z, a, h),
+                    s2[p].at[u, EARLY, h], r2[p].at[u, EARLY, slot], u, F2 + p, dev(yl_to, z, a, h),
                     a == core if d == 0 and yl_to is yl else None,
                 )
 
-    def send_late(u, t, a, slot):
+    def send_late(u, p, a, slot):
         for d in FAR:
             h = lax.rem(g + d, NG)
             for core_to in (core, mate):
                 send(
-                    s2.at[u, LATE, t, h], r2.at[u, LATE, t, slot], u, F2 + 2 + t, dev(a, z, core_to, h),
+                    s2[p].at[u, LATE, h], r2[p].at[u, LATE, slot], u, F2 + 3 + p, dev(a, z, core_to, h),
                     a == yl if d == 0 and core_to is core else None,
                 )
 
-    def assemble(u, e, h):
+    def assemble(u, e, p):
         n_src, n_g = (2, 8) if u == 0 else (4, 4)
         to = y0 if u == 0 else y1
         for s in range(n_src):
             for q in range(n_g // 2):
-                for t in range(2):
+                for t in range(PIECES[p][1]):
                     at = slice(128 * t, 128 * t + 128)
-                    even, other = r2[u, e, h, s * n_g + 2 * q, :, at], r2[u, e, h, s * n_g + 2 * q + 1, :, at]
-                    r = 4 * h + 2 * t
+                    even, other = r2[p][u, e, s * n_g + 2 * q, :, at], r2[p][u, e, s * n_g + 2 * q + 1, :, at]
+                    r = 2 * (PIECES[p][0] + t)
                     if u == 1:
                         row = (s * ROWS + r) * NZ
                     else:
-                        row = (s * 4 + r if h == 0 else 8 + s * 3 + r - 4) * NZ
+                        row = (s * 4 + r if r < 4 else 8 + s * 3 + r - 4) * NZ
                     to_lanes = slice(128 * q, 128 * q + 128)
                     to[e, row : row + NZ, to_lanes] = jnp.where(low, even, other)
                     if r + 1 < ROWS:
@@ -218,24 +225,25 @@
         if u == 0:
             push(u, 1)
 
-        for h in range(2):
-            wait_all(r1.at[u, h], rsem.at[u, F1 + h])
-            channels_apart(u, h)
-            send_early(u, h, a, slot)
-            send_late(u, h, a, slot)
-
-        for e in (EARLY, LATE):
-            wait_all(r2.at[u, e, 0], rsem.at[u, F2 + 2 * e])
-            assemble(u, e, 0)
-        wait_all(r2.at[u, EARLY, 1], rsem.at[u, F2 + 1])
-        assemble(u, EARLY, 1)
+        for p in range(3):
+            wait_all(r1[p].at[u], rsem.at[u, F1 + p])
+            channels_apart(u, p)
+            send_early(u, p, a, slot)
+            send_late(u, p, a, slot)
+
+        for p in range(2):
+            for e in (EARLY, LATE):
+                wait_all(r2[p].at[u, e], rsem.at[u, F2 + 3 * e + p])
+                assemble(u, e, p)
+        wait_all(r2[2].at[u, EARLY], rsem.at[u, F2 + 2])
+        assemble(u, EARLY, 2)
         if u == 0:
             e0[...] = mm(y0[EARLY], cols[...], 0, 0).astype(BF16)
         else:
             e1[...] = mm(cols[...], y1[EARLY], 1, 1).astype(BF16)
 
-        wait_all(r2.at[u, LATE, 1], rsem.at[u, F2 + 3])
-        assemble(u, LATE, 1)
+        wait_all(r2[2].at[u, LATE], rsem.at[u, F2 + 5])
+        assemble(u, LATE, 2)
 
         i_half, j_half = (yl, core) if u == 0 else (core, yl)
         for h in range(2):
@@ -277,10 +285,10 @@
             if u == 0:
                 norm(h)
                 push(1, h)
-
-    ztok[...] = zt[...].T
-    for r in range(ROWS):
-        out_ref[r] = ztok[slot_rows(r), :].astype(BF16)
+            else:
+                ztok[lanes(h), :] = zt[:, lanes(h)].T
+                for r in range(4 * h, min(4 * h + 4, ROWS)):
+                    out_ref[r] = ztok[slot_rows(r), :].astype(BF16)
 
     def wait_sent(u, stage, ref, count, less):
         @pl.when(less)
@@ -293,11 +301,11 @@
 
     for u in range(2):
         a = yl if u == 0 else g // 4
+        for p in range(3):
+            wait_all(s1[p].at[u, pl.ds(0, NZ - 1)], ssem.at[u, F1 + p])
+            wait_sent(u, F2 + p, r2[p].at[u, EARLY], 2 * NG, a == core)
+            wait_sent(u, F2 + 3 + p, r2[p].at[u, LATE], 2 * NG, a == yl)
         for h in range(2):
-            wait_all(s1.at[u, h, pl.ds(0, NZ - 1)], ssem.at[u, F1 + h])
-        for h in range(2):
-            wait_sent(u, F2 + h, r2.at[u, EARLY, h], 2 * NG, a == core)
-            wait_sent(u, F2 + 2 + h, r2.at[u, LATE, h], 2 * NG, a == yl)
             wait_sent(u, B1 + h, s3.at[u, h], 8, g // 4 == core if u == 0 else (core == yl) & (g // 4 == yl))
             wait_all(s4.at[u, h, pl.ds(0, NZ - 1)], ssem.at[u, B2 + h])
 
@@ -323,10 +331,10 @@
             pltpu.VMEM((CH, TOK), F32),
             pltpu.VMEM((CH, TOK), BF16),
             pltpu.VMEM((CH, TOK), F32),
-            pltpu.VMEM((2, 2, NZ, 16, HALF), BF16),
-            pltpu.VMEM((2, 2, NZ, 16, HALF), BF16),
-            pltpu.VMEM((2, 2, 2, NG, NZ, HALF), BF16),
-            pltpu.VMEM((2, 2, 2, 16, NZ, HALF), BF16),
+            *(pltpu.VMEM((2, NZ, 16, 128 * n), BF16) for _, n in PIECES),
+            *(pltpu.VMEM((2, NZ, 16, 128 * n), BF16) for _, n in PIECES),
+            *(pltpu.VMEM((2, 2, NG, NZ, 128 * n), BF16) for _, n in PIECES),
+            *(pltpu.VMEM((2, 2, 16, NZ, 128 * n), BF16) for _, n in PIECES),
             pltpu.VMEM((2, 224, 512), BF16),
             pltpu.VMEM((2, 448, 256), BF16),
             pltpu.VMEM((512, 256), BF16),

time: 86 us -> 86.9 us (1.010)
  no operation moved by 1% of the time
where the time goes in v5:
time: 86.9 us; the launch traced here: 85.3 us
  Pallas kernels  84.6 us (97%)
    pallas_call x1, Pallas kernels, body(): pl.pallas_call(kernel, out_shape=pltpu.VMEM(pair.shape, pair.dtype), in_s...  84.6 us

profile of v5, /device:TPU:24, one launch (start us, length us, event | category | flops | bytes accessed | tf_op | source)
XLA Modules:
  0.0 85.3 jit_solution(13489977459260453604)
XLA Ops:
  0.0 84.6 %triangle.1 = bf16[7,56,128]{2,1,0:T(8,128)(2,1)S(1)} custom-call(bf16[7,56,128]{2,1,0:T(8,128)(2,1)} %pair_hbm.1, s32[7,56]{1,0:T(8,128)} %mask_hbm.1, bf16[2,128,512]{2,1,0:T(8,128)(2,1)} %wab_hbm.1, bf16[2,128,128]{2,1,0:T(8,128)(2,1)} %wg_hbm.1, bf16[2,128,128]{2,1,0:T(8,128)(2,1)} %wo_hbm.1), custom_call_target="tpu_custom_call" | custom-call | tf_op jit(solution)/shard_map/triangle/pallas_call | solution.py:314
  84.6 0.6 copy.7

commit v6 on v4

--- a/solution.py
+++ b/solution.py
@@ -45,7 +45,7 @@
 def kernel(
     pair_hbm, mask_hbm, wab_hbm, wg_hbm, wo_hbm, out_ref,
     pair_ref, mask_ref, wab_ref, wg_ref, wo_ref, wabt, wgt, wot, perm, cols,
-    ztok, zt, zn, gate, s1, r1, s2, r2, y0, y1, e0, e1, s3, r3, s4, r4, insem, ssem, rsem,
+    ztok, zt, zn, gate, s1, r1, s2, r2, y0, y1, e0, e1, part0, part1, s3, r3, s4, r4, insem, ssem, rsem,
 ):
     loads = [
         pltpu.make_async_copy(src, dst, insem.at[n])
@@ -190,10 +190,7 @@
                     at = slice(128 * t, 128 * t + 128)
                     even, other = r2[u, e, h, s * n_g + 2 * q, :, at], r2[u, e, h, s * n_g + 2 * q + 1, :, at]
                     r = 4 * h + 2 * t
-                    if u == 1:
-                        row = (s * ROWS + r) * NZ
-                    else:
-                        row = (s * 4 + r if h == 0 else 8 + s * 3 + r - 4) * NZ
+                    row = (s * 4 + r if h == 0 else n_src * 4 + s * 3 + r - 4) * NZ
                     to_lanes = slice(128 * q, 128 * q + 128)
                     to[e, row : row + NZ, to_lanes] = jnp.where(low, even, other)
                     if r + 1 < ROWS:
@@ -227,24 +224,29 @@
         for e in (EARLY, LATE):
             wait_all(r2.at[u, e, 0], rsem.at[u, F2 + 2 * e])
             assemble(u, e, 0)
+        if u == 0:
+            part0[...] = mm(y0[EARLY, :128], cols[:128], 0, 0)
+        else:
+            e1[:, :256] = mm(cols[...], y1[EARLY, :256], 1, 1).astype(BF16)
+            part1[...] = mm(e1[:, :256], y1[LATE, :256])
         wait_all(r2.at[u, EARLY, 1], rsem.at[u, F2 + 1])
         assemble(u, EARLY, 1)
         if u == 0:
-            e0[...] = mm(y0[EARLY], cols[...], 0, 0).astype(BF16)
+            e0[...] = (part0[...] + mm(y0[EARLY, 128:], cols[128:], 0, 0)).astype(BF16)
         else:
-            e1[...] = mm(cols[...], y1[EARLY], 1, 1).astype(BF16)
-
-        wait_all(r2.at[u, LATE, 1], rsem.at[u, F2 + 3])
-        assemble(u, LATE, 1)
+            e1[:, 256:] = mm(cols[...], y1[EARLY, 256:], 1, 1).astype(BF16)
 
         i_half, j_half = (yl, core) if u == 0 else (core, yl)
         for h in range(2):
             n_r = 4 - h
             rows = slice(128 * h, 128 * h + 32 * n_r)
+            if h == 1 - u:
+                wait_all(r2.at[u, LATE, 1], rsem.at[u, F2 + 3])
+                assemble(u, LATE, 1)
             if u == 0:
                 tri = mm(y0[LATE, rows, :], e0[...]).astype(BF16)
             else:
-                tri = mm(e1[rows, :], y1[LATE]).astype(BF16)
+                tri = (part1[rows, :] + mm(e1[rows, 256:], y1[LATE, 256:])).astype(BF16)
             for ci in range(2):
                 for t in range(2):
                     for q in range(2):
@@ -277,10 +279,10 @@
             if u == 0:
                 norm(h)
                 push(1, h)
-
-    ztok[...] = zt[...].T
-    for r in range(ROWS):
-        out_ref[r] = ztok[slot_rows(r), :].astype(BF16)
+            else:
+                ztok[lanes(h), :] = zt[:, lanes(h)].T
+                for r in range(4 * h, min(4 * h + 4, ROWS)):
+                    out_ref[r] = ztok[slot_rows(r), :].astype(BF16)
 
     def wait_sent(u, stage, ref, count, less):
         @pl.when(less)
@@ -331,6 +333,8 @@
             pltpu.VMEM((2, 448, 256), BF16),
             pltpu.VMEM((512, 256), BF16),
             pltpu.VMEM((224, 448), BF16),
+            pltpu.VMEM((512, 256), F32),
+            pltpu.VMEM((224, 256), F32),
             pltpu.VMEM((2, 2, 8, NZ, HALF), BF16),
             pltpu.VMEM((2, 2, 8, NZ, HALF), BF16),
             pltpu.VMEM((2, 2, NZ, 16, 128), BF16),

time: 86 us -> 86 us (level)
  no operation moved by 1% of the time
where the time goes in v6:
time: 86 us; the launch traced here: 84.4 us
  Pallas kernels  83.7 us (97%)
    pallas_call x1, Pallas kernels, body(): pl.pallas_call(kernel, out_shape=pltpu.VMEM(pair.shape, pair.dtype), in_s...  83.7 us

profile of v6, /device:TPU:24, one launch (start us, length us, event | category | flops | bytes accessed | tf_op | source)
XLA Modules:
  0.0 84.4 jit_solution(7684622153676903576)
XLA Ops:
  0.0 83.7 %triangle.1 = bf16[7,56,128]{2,1,0:T(8,128)(2,1)S(1)} custom-call(bf16[7,56,128]{2,1,0:T(8,128)(2,1)} %pair_hbm.1, s32[7,56]{1,0:T(8,128)} %mask_hbm.1, bf16[2,128,512]{2,1,0:T(8,128)(2,1)} %wab_hbm.1, bf16[2,128,128]{2,1,0:T(8,128)(2,1)} %wg_hbm.1, bf16[2,128,128]{2,1,0:T(8,128)(2,1)} %wo_hbm.1), custom_call_target="tpu_custom_call" | custom-call | tf_op jit(solution)/shard_map/triangle/pallas_call | solution.py:308
  83.7 0.6 copy.7

commit v7 on v6

--- a/solution.py
+++ b/solution.py
@@ -13,7 +13,7 @@
 AROUND = (8, 7, 9, 6, 10, 5, 11, 4, 12, 3, 13, 2, 14, 1, 15)
 FAR = (6, 5, 7, 2, 4, 1, 3, 0)
 EARLY, LATE = 0, 1
-F1, F2, B1, B2, STAGES = 0, 2, 6, 8, 10
+F1, F2, MATE, B1, B2, STAGES = 0, 2, 6, 8, 10, 12
 
 
 def mm(a, b, ca=1, cb=0):
@@ -175,26 +175,33 @@
     def send_late(u, t, a, slot):
         for d in FAR:
             h = lax.rem(g + d, NG)
-            for core_to in (core, mate):
-                send(
-                    s2.at[u, LATE, t, h], r2.at[u, LATE, t, slot], u, F2 + 2 + t, dev(a, z, core_to, h),
-                    a == yl if d == 0 and core_to is core else None,
-                )
-
-    def assemble(u, e, h):
-        n_src, n_g = (2, 8) if u == 0 else (4, 4)
+            send(
+                s2.at[u, LATE, t, h], r2.at[u, LATE, t, slot], u, F2 + 2 + t, dev(a, z, core, h),
+                a == yl if d == 0 else None,
+            )
+
+    def hand_over(u, t):
+        own = r2.at[u, LATE, t, pl.ds(core * NG, NG)]
+        wait_all(own, rsem.at[u, F2 + 2 + t])
+        send(own, own, u, MATE + t, dev(yl, z, mate, g))
+
+    def assemble(u, e, h, cs):
+        n_src, n_g = (1, 8) if u == 0 else (2, 4)
         to = y0 if u == 0 else y1
         for s in range(n_src):
             for q in range(n_g // 2):
                 for t in range(2):
                     at = slice(128 * t, 128 * t + 128)
-                    even, other = r2[u, e, h, s * n_g + 2 * q, :, at], r2[u, e, h, s * n_g + 2 * q + 1, :, at]
+                    slot, source = cs * NG + s * n_g + 2 * q, cs * n_src + s
+                    even, other = r2[u, e, h, slot, :, at], r2[u, e, h, slot + 1, :, at]
                     r = 4 * h + 2 * t
-                    row = (s * 4 + r if h == 0 else n_src * 4 + s * 3 + r - 4) * NZ
+                    row = (source * 4 + r if h == 0 else n_src * 8 + source * 3 + r - 4) * NZ
                     to_lanes = slice(128 * q, 128 * q + 128)
-                    to[e, row : row + NZ, to_lanes] = jnp.where(low, even, other)
+                    if not isinstance(cs, int):
+                        row = pl.multiple_of(row, NZ)
+                    to[e, pl.ds(row, NZ), to_lanes] = jnp.where(low, even, other)
                     if r + 1 < ROWS:
-                        to[e, row + NZ : row + 2 * NZ, to_lanes] = pltpu.roll(jnp.where(low, other, even), 64, 1)
+                        to[e, pl.ds(row + NZ, NZ), to_lanes] = pltpu.roll(jnp.where(low, other, even), 64, 1)
 
     def finish(u, h):
         x = r4[u, h].astype(F32).reshape(NZ, 2, NG, 128)
@@ -221,16 +228,21 @@
             send_early(u, h, a, slot)
             send_late(u, h, a, slot)
 
-        for e in (EARLY, LATE):
-            wait_all(r2.at[u, e, 0], rsem.at[u, F2 + 2 * e])
-            assemble(u, e, 0)
+        hand_over(u, 0)
+        wait_all(r2.at[u, EARLY, 0], rsem.at[u, F2])
+        assemble(u, EARLY, 0, 0)
+        assemble(u, EARLY, 0, 1)
+        wait_all(r2.at[u, LATE, 0, pl.ds(0, NG)], rsem.at[u, MATE])
+        assemble(u, LATE, 0, 0)
+        assemble(u, LATE, 0, 1)
         if u == 0:
             part0[...] = mm(y0[EARLY, :128], cols[:128], 0, 0)
         else:
             e1[:, :256] = mm(cols[...], y1[EARLY, :256], 1, 1).astype(BF16)
             part1[...] = mm(e1[:, :256], y1[LATE, :256])
         wait_all(r2.at[u, EARLY, 1], rsem.at[u, F2 + 1])
-        assemble(u, EARLY, 1)
+        assemble(u, EARLY, 1, 0)
+        assemble(u, EARLY, 1, 1)
         if u == 0:
             e0[...] = (part0[...] + mm(y0[EARLY, 128:], cols[128:], 0, 0)).astype(BF16)
         else:
@@ -241,8 +253,10 @@
             n_r = 4 - h
             rows = slice(128 * h, 128 * h + 32 * n_r)
             if h == 1 - u:
-                wait_all(r2.at[u, LATE, 1], rsem.at[u, F2 + 3])
-                assemble(u, LATE, 1)
+                hand_over(u, 1)
+                assemble(u, LATE, 1, core)
+                wait_all(r2.at[u, LATE, 1, pl.ds(0, NG)], rsem.at[u, MATE + 1])
+                assemble(u, LATE, 1, mate)
             if u == 0:
                 tri = mm(y0[LATE, rows, :], e0[...]).astype(BF16)
             else:
@@ -299,7 +313,8 @@
             wait_all(s1.at[u, h, pl.ds(0, NZ - 1)], ssem.at[u, F1 + h])
         for h in range(2):
             wait_sent(u, F2 + h, r2.at[u, EARLY, h], 2 * NG, a == core)
-            wait_sent(u, F2 + 2 + h, r2.at[u, LATE, h], 2 * NG, a == yl)
+            wait_sent(u, F2 + 2 + h, r2.at[u, LATE, h], NG, a == yl)
+            wait_all(r2.at[u, LATE, h, pl.ds(0, NG)], ssem.at[u, MATE + h])
             wait_sent(u, B1 + h, s3.at[u, h], 8, g // 4 == core if u == 0 else (core == yl) & (g // 4 == yl))
             wait_all(s4.at[u, h, pl.ds(0, NZ - 1)], ssem.at[u, B2 + h])
 

time: 86 us -> 85.2 us (level); the launches traced: 84.4 us -> 85.1 us
  no operation moved by 1% of the time
where the time goes in v7:
time: 85.2 us; the launch traced here: 85.1 us
  Pallas kernels  84.4 us (99%)
    pallas_call x1, Pallas kernels, body(): pl.pallas_call(kernel, out_shape=pltpu.VMEM(pair.shape, pair.dtype), in_s...  84.4 us

profile of v7, /device:TPU:24, one launch (start us, length us, event | category | flops | bytes accessed | tf_op | source)
XLA Modules:
  0.0 85.1 jit_solution(13173872311314837177)
XLA Ops:
  0.0 84.4 %triangle.1 = bf16[7,56,128]{2,1,0:T(8,128)(2,1)S(1)} custom-call(bf16[7,56,128]{2,1,0:T(8,128)(2,1)} %pair_hbm.1, s32[7,56]{1,0:T(8,128)} %mask_hbm.1, bf16[2,128,512]{2,1,0:T(8,128)(2,1)} %wab_hbm.1, bf16[2,128,128]{2,1,0:T(8,128)(2,1)} %wg_hbm.1, bf16[2,128,128]{2,1,0:T(8,128)(2,1)} %wo_hbm.1), custom_call_target="tpu_custom_call" | custom-call | tf_op jit(solution)/shard_map/triangle/pallas_call | solution.py:323
  84.4 0.6 copy.7

commit v8 on v7

--- a/solution.py
+++ b/solution.py
@@ -127,7 +127,7 @@
     loads[0].wait()
     for r in range(ROWS):
         ztok[slot_rows(r), :] = pair_ref[r].astype(F32)
-    zt[...] = ztok[...].T
+    zt[:, :HALF] = ztok[:HALF].T
 
     def lanes(h):
         return slice(HALF * h, HALF * h + HALF)
@@ -158,10 +158,9 @@
         ri = jnp.where(n < 8, lax.rem(n, 4), 4 + lax.rem(n - 8, 3))
         cols[...] = one_hot(l == zi // 4 * MS + lax.rem(zi, 4) * 14 + ci * 7 + ri)
 
-    def channels_apart(u, h):
-        x = mm(perm[...], r1[u, h].reshape(256, HALF)).astype(BF16)
-        for e in (EARLY, LATE):
-            s2[u, e, h] = x[128 * e : 128 * e + 128].reshape(NG, NZ, HALF)
+    def channels_apart(u, h, e):
+        x = mm(perm[128 * e : 128 * e + 128], r1[u, h].reshape(256, HALF)).astype(BF16)
+        s2[u, e, h] = x.reshape(NG, NZ, HALF)
 
     def send_early(u, t, a, slot):
         for d in FAR:
@@ -216,16 +215,19 @@
             norm(0)
             pl.semaphore_wait(barrier, NZ - 1 + 4 * NG - 1)
             push(u, 0)
+            zt[:, HALF:] = ztok[HALF:].T
             norm(1)
             constants()
         gate[...] = sigmoid(mm(wgt[u], zn[...]))
         if u == 0:
+            wait_all(s1.at[u, 0, pl.ds(0, NZ - 1)], ssem.at[u, F1])
             push(u, 1)
 
         for h in range(2):
             wait_all(r1.at[u, h], rsem.at[u, F1 + h])
-            channels_apart(u, h)
+            channels_apart(u, h, EARLY)
             send_early(u, h, a, slot)
+            channels_apart(u, h, LATE)
             send_late(u, h, a, slot)
 
         hand_over(u, 0)
@@ -310,7 +312,8 @@
     for u in range(2):
         a = yl if u == 0 else g // 4
         for h in range(2):
-            wait_all(s1.at[u, h, pl.ds(0, NZ - 1)], ssem.at[u, F1 + h])
+            if u == 1 or h == 1:
+                wait_all(s1.at[u, h, pl.ds(0, NZ - 1)], ssem.at[u, F1 + h])
         for h in range(2):
             wait_sent(u, F2 + h, r2.at[u, EARLY, h], 2 * NG, a == core)
             wait_sent(u, F2 + 2 + h, r2.at[u, LATE, h], NG, a == yl)

time: 85.2 us -> 85.7 us (level); the launches traced: 85.1 us -> 84.5 us
  no operation moved by 1% of the time
where the time goes in v8:
time: 85.7 us; the launch traced here: 84.5 us
  Pallas kernels  83.8 us (98%)
    pallas_call x1, Pallas kernels, body(): pl.pallas_call(kernel, out_shape=pltpu.VMEM(pair.shape, pair.dtype), in_s...  83.8 us

profile of v8, /device:TPU:24, one launch (start us, length us, event | category | flops | bytes accessed | tf_op | source)
XLA Modules:
  0.0 84.5 jit_solution(6706779949052799423)
XLA Ops:
  0.0 83.8 %triangle.1 = bf16[7,56,128]{2,1,0:T(8,128)(2,1)S(1)} custom-call(bf16[7,56,128]{2,1,0:T(8,128)(2,1)} %pair_hbm.1, s32[7,56]{1,0:T(8,128)} %mask_hbm.1, bf16[2,128,512]{2,1,0:T(8,128)(2,1)} %wab_hbm.1, bf16[2,128,128]{2,1,0:T(8,128)(2,1)} %wg_hbm.1, bf16[2,128,128]{2,1,0:T(8,128)(2,1)} %wo_hbm.1), custom_call_target="tpu_custom_call" | custom-call | tf_op jit(solution)/shard_map/triangle/pallas_call | solution.py:326
  83.8 0.6 copy.7

commit v9 on v7

--- a/solution.py
+++ b/solution.py
@@ -13,7 +13,7 @@
 AROUND = (8, 7, 9, 6, 10, 5, 11, 4, 12, 3, 13, 2, 14, 1, 15)
 FAR = (6, 5, 7, 2, 4, 1, 3, 0)
 EARLY, LATE = 0, 1
-F1, F2, MATE, B1, B2, STAGES = 0, 2, 6, 8, 10, 12
+F1, F2, MATE, B1, B2, TAIL, STAGES = 0, 2, 6, 8, 10, 12, 13
 
 
 def mm(a, b, ca=1, cb=0):
@@ -44,7 +44,7 @@
 
 def kernel(
     pair_hbm, mask_hbm, wab_hbm, wg_hbm, wo_hbm, out_ref,
-    pair_ref, mask_ref, wab_ref, wg_ref, wo_ref, wabt, wgt, wot, perm, cols,
+    pair_ref, mask_ref, wab_ref, wg_ref, wo_ref, wabt, wgt, wot, perm, cols, padded, s1d, r1d, st, rt, dense0,
     ztok, zt, zn, gate, s1, r1, s2, r2, y0, y1, e0, e1, part0, part1, s3, r3, s4, r4, insem, ssem, rsem,
 ):
     loads = [
@@ -121,13 +121,16 @@
     loads[2].wait()
     spread = mm(mask_ref[...].astype(F32).astype(BF16), places)
     keep = jnp.sum(jnp.where(l // MS == k + odd * (1 - 2 * lax.rem(k, 2)), spread, 0.0), axis=0, keepdims=True)
+    kc, lc = iota2((COLS, TOK))
+    spread = mm(mask_ref[...].astype(F32).astype(BF16), one_hot(lax.rem(lc, COLS) == kc))
+    keep_dense = jnp.sum(jnp.where(l // COLS == k, spread, 0.0), axis=0, keepdims=True)
 
     loads[1].wait()
     wabt[0] = wab_ref[0].T
     loads[0].wait()
     for r in range(ROWS):
-        ztok[slot_rows(r), :] = pair_ref[r].astype(F32)
-    zt[...] = ztok[...].T
+        ztok[r * COLS : r * COLS + COLS, :] = pair_ref[r].astype(F32)
+    zn[...] = normalize(ztok[...].T, (0,)).astype(BF16)
 
     def lanes(h):
         return slice(HALF * h, HALF * h + HALF)
@@ -143,6 +146,47 @@
         left, right = side(0), side(2 * CH)
         s1[u, h] = jnp.concatenate([right, left] if u == 0 else [left, right], axis=1).astype(BF16)
         send_z(s1.at[u, h], r1.at[u, h], u, F1 + h)
+
+    def push_dense():
+        def side(base):
+            p = mm(wabt[0, base : base + 2 * CH, :], zn[...])
+            return sigmoid(p[:CH]) * p[CH:] * keep_dense
+
+        both = side(2 * CH), side(0)
+        s1[0, 0] = jnp.concatenate([x[:, :256].reshape(NZ, NG, 256) for x in both], axis=1).astype(BF16)
+        send_z(s1.at[0, 0], r1.at[0, 0], 0, F1)
+        k, l = iota2((128, 128))
+        spread_out = one_hot((k < 8) & (lax.rem(l, 8) == k))
+        c = lax.broadcasted_iota(jnp.int32, (NZ, NG, 128), 1)
+        l = lax.broadcasted_iota(jnp.int32, (NZ, NG, 128), 2)
+        tail = jnp.zeros((NZ, 1, 128), F32)
+        for e in (EARLY, LATE):
+            x = mm(both[e][:, 384:].astype(BF16), spread_out).reshape(NZ, NG, 128)
+            tail = tail + jnp.sum(jnp.where(l // 8 == e * NG + c, x, 0.0), axis=1, keepdims=True)
+        st[...] = tail
+        s1d[...] = jnp.concatenate([x[:, 256:384].reshape(NZ, NG, 128) for x in both], axis=1).astype(BF16)
+
+    def push_rest():
+        send_z(st, rt, 0, TAIL)
+        send_z(s1d, r1d, 0, F1 + 1)
+
+    def tail_of(e):
+        c = lax.broadcasted_iota(jnp.int32, (NG, NZ, 128), 0)
+        l = lax.broadcasted_iota(jnp.int32, (NG, NZ, 128), 2)
+        x = jnp.broadcast_to(rt[...].reshape(1, NZ, 128), (NG, NZ, 128))
+        return jnp.where(l // 8 == e * NG + c, x, 0.0).reshape(CH, 128).astype(BF16)
+
+    def channels_apart_dense(h):
+        if h == 0:
+            x = mm(perm[...], r1[0, 0].reshape(256, HALF)).astype(BF16)
+            dense0[...] = x
+            x = mm(x, padded[:HALF, :HALF]).astype(BF16)
+        else:
+            x = mm(perm[...], r1d[...].reshape(256, 128)).astype(BF16)
+            tails = jnp.concatenate([tail_of(EARLY), tail_of(LATE)], axis=0)
+            x = mm(jnp.concatenate([dense0[...], x, tails], axis=1), padded[:, HALF:]).astype(BF16)
+        for e in (EARLY, LATE):
+            s2[0, e, h] = x[128 * e : 128 * e + 128].reshape(NG, NZ, HALF)
 
     def constants():
         for load in loads[3:]:
@@ -157,6 +201,11 @@
         ci = jnp.where(n < 8, n // 4, (n - 8) // 3)
         ri = jnp.where(n < 8, lax.rem(n, 4), 4 + lax.rem(n - 8, 3))
         cols[...] = one_hot(l == zi // 4 * MS + lax.rem(zi, 4) * 14 + ci * 7 + ri)
+        t = lax.broadcasted_iota(jnp.int32, (TOK, 1), 0)
+        t = jnp.where(t < 384, t, 384 + lax.rem(t, 8))
+        r = t // COLS
+        spot = (r + odd * (1 - 2 * lax.rem(r, 2))) * MS + lax.rem(t, COLS)
+        padded[...] = one_hot(lax.broadcasted_iota(jnp.int32, (TOK, TOK), 1) == spot)
 
     def channels_apart(u, h):
         x = mm(perm[...], r1[u, h].reshape(256, HALF)).astype(BF16)
@@ -213,18 +262,28 @@
         a = yl if u == 0 else g // 4
         slot = core * NG + g if u == 0 else (core * 2 + yl) * 4 + lax.rem(g, 4)
         if u == 0:
+            pl.semaphore_wait(barrier, NZ - 1 + 4 * NG - 1)
+            push_dense()
+            constants()
+            push_rest()
+            ztok[...] = jnp.zeros_like(ztok)
+            for r in range(ROWS):
+                ztok[slot_rows(r), :] = pair_ref[r].astype(F32)
+            zt[...] = ztok[...].T
             norm(0)
-            pl.semaphore_wait(barrier, NZ - 1 + 4 * NG - 1)
-            push(u, 0)
             norm(1)
-            constants()
         gate[...] = sigmoid(mm(wgt[u], zn[...]))
-        if u == 0:
-            push(u, 1)
-
-        for h in range(2):
-            wait_all(r1.at[u, h], rsem.at[u, F1 + h])
-            channels_apart(u, h)
+
+        for h in range(2):
+            if u == 0 and h == 1:
+                wait_all(rt, rsem.at[u, TAIL])
+                wait_all(r1d, rsem.at[u, F1 + 1])
+            else:
+                wait_all(r1.at[u, h], rsem.at[u, F1 + h])
+            if u == 0:
+                channels_apart_dense(h)
+            else:
+                channels_apart(u, h)
             send_early(u, h, a, slot)
             send_late(u, h, a, slot)
 
@@ -310,7 +369,11 @@
     for u in range(2):
         a = yl if u == 0 else g // 4
         for h in range(2):
-            wait_all(s1.at[u, h, pl.ds(0, NZ - 1)], ssem.at[u, F1 + h])
+            if u == 0 and h == 1:
+                wait_all(st.at[pl.ds(0, NZ - 1)], ssem.at[u, TAIL])
+                wait_all(s1d.at[pl.ds(0, NZ - 1)], ssem.at[u, F1 + 1])
+            else:
+                wait_all(s1.at[u, h, pl.ds(0, NZ - 1)], ssem.at[u, F1 + h])
         for h in range(2):
             wait_sent(u, F2 + h, r2.at[u, EARLY, h], 2 * NG, a == core)
             wait_sent(u, F2 + 2 + h, r2.at[u, LATE, h], NG, a == yl)
@@ -336,6 +399,12 @@
             pltpu.VMEM((2, CH, CH), BF16),
             pltpu.VMEM((256, 256), BF16),
             pltpu.VMEM((224, 256), BF16),
+            pltpu.VMEM((TOK, TOK), BF16),
+            pltpu.VMEM((NZ, 16, 128), BF16),
+            pltpu.VMEM((NZ, 16, 128), BF16),
+            pltpu.VMEM((NZ, 1, 128), F32),
+            pltpu.VMEM((NZ, 1, 128), F32),
+            pltpu.VMEM((256, 256), BF16),
             pltpu.VMEM((TOK, CH), F32),
             pltpu.VMEM((CH, TOK), F32),
             pltpu.VMEM((CH, TOK), BF16),

time: 85.2 us -> 83.9 us (0.985)
  Pallas kernels: 84.4 us -> 82.9 us
    pallas_call x1, Pallas kernels: 84.4 us -> 82.9 us  [body(): pl.pallas_call(kernel, out_shape=pltpu.VMEM(pair.shape, pair.dtype), in_s...]
where the time goes in v9:
time: 83.9 us; the launch traced here: 83.6 us
  Pallas kernels  82.9 us (99%)
    pallas_call x1, Pallas kernels, body(): pl.pallas_call(kernel, out_shape=pltpu.VMEM(pair.shape, pair.dtype), in_s...  82.9 us

profile of v9, /device:TPU:24, one launch (start us, length us, event | category | flops | bytes accessed | tf_op | source)
XLA Modules:
  0.0 83.6 jit_solution(6694569733237288254)
XLA Ops:
  0.0 82.9 %triangle.1 = bf16[7,56,128]{2,1,0:T(8,128)(2,1)S(1)} custom-call(bf16[7,56,128]{2,1,0:T(8,128)(2,1)} %pair_hbm.1, s32[7,56]{1,0:T(8,128)} %mask_hbm.1, bf16[2,128,512]{2,1,0:T(8,128)(2,1)} %wab_hbm.1, bf16[2,128,128]{2,1,0:T(8,128)(2,1)} %wg_hbm.1, bf16[2,128,128]{2,1,0:T(8,128)(2,1)} %wo_hbm.1), custom_call_target="tpu_custom_call" | custom-call | tf_op jit(solution)/shard_map/triangle/pallas_call | solution.py:386
  82.9 0.6 copy.7

commit v10 on v9

--- a/solution.py
+++ b/solution.py
@@ -148,23 +148,24 @@
         send_z(s1.at[u, h], r1.at[u, h], u, F1 + h)
 
     def push_dense():
-        def side(base):
-            p = mm(wabt[0, base : base + 2 * CH, :], zn[...])
-            return sigmoid(p[:CH]) * p[CH:] * keep_dense
-
-        both = side(2 * CH), side(0)
-        s1[0, 0] = jnp.concatenate([x[:, :256].reshape(NZ, NG, 256) for x in both], axis=1).astype(BF16)
+        def side(base, h):
+            p = mm(wabt[0, base : base + 2 * CH, :], zn[:, lanes(h)])
+            return sigmoid(p[:CH]) * p[CH:] * keep_dense[:, lanes(h)]
+
+        both = side(2 * CH, 0), side(0, 0)
+        s1[0, 0] = jnp.concatenate([x.reshape(NZ, NG, 256) for x in both], axis=1).astype(BF16)
         send_z(s1.at[0, 0], r1.at[0, 0], 0, F1)
+        both = side(2 * CH, 1), side(0, 1)
         k, l = iota2((128, 128))
         spread_out = one_hot((k < 8) & (lax.rem(l, 8) == k))
         c = lax.broadcasted_iota(jnp.int32, (NZ, NG, 128), 1)
         l = lax.broadcasted_iota(jnp.int32, (NZ, NG, 128), 2)
         tail = jnp.zeros((NZ, 1, 128), F32)
         for e in (EARLY, LATE):
-            x = mm(both[e][:, 384:].astype(BF16), spread_out).reshape(NZ, NG, 128)
+            x = mm(both[e][:, 128:].astype(BF16), spread_out).reshape(NZ, NG, 128)
             tail = tail + jnp.sum(jnp.where(l // 8 == e * NG + c, x, 0.0), axis=1, keepdims=True)
         st[...] = tail
-        s1d[...] = jnp.concatenate([x[:, 256:384].reshape(NZ, NG, 128) for x in both], axis=1).astype(BF16)
+        s1d[...] = jnp.concatenate([x[:, :128].reshape(NZ, NG, 128) for x in both], axis=1).astype(BF16)
 
     def push_rest():
         send_z(st, rt, 0, TAIL)
@@ -266,13 +267,6 @@
             push_dense()
             constants()
             push_rest()
-            ztok[...] = jnp.zeros_like(ztok)
-            for r in range(ROWS):
-                ztok[slot_rows(r), :] = pair_ref[r].astype(F32)
-            zt[...] = ztok[...].T
-            norm(0)
-            norm(1)
-        gate[...] = sigmoid(mm(wgt[u], zn[...]))
 
         for h in range(2):
             if u == 0 and h == 1:
@@ -286,6 +280,15 @@
                 channels_apart(u, h)
             send_early(u, h, a, slot)
             send_late(u, h, a, slot)
+            if h == 0:
+                if u == 0:
+                    ztok[...] = jnp.zeros_like(ztok)
+                    for r in range(ROWS):
+                        ztok[slot_rows(r), :] = pair_ref[r].astype(F32)
+                    zt[...] = ztok[...].T
+                    norm(0)
+                    norm(1)
+                gate[...] = sigmoid(mm(wgt[u], zn[...]))
 
         hand_over(u, 0)
         wait_all(r2.at[u, EARLY, 0], rsem.at[u, F2])

time: 83.9 us -> 85.2 us (1.015)
  the two profiles are of different devices: /device:TPU:24 before, /device:TPU:1 now
where the time goes in v10:
time: 85.2 us; the launch traced here: 85.1 us
  Pallas kernels  84.4 us (99%)
    pallas_call x1, Pallas kernels, body(): pl.pallas_call(kernel, out_shape=pltpu.VMEM(pair.shape, pair.dtype), in_s...  84.4 us

profile of v10, /device:TPU:1, one launch (start us, length us, event | category | flops | bytes accessed | tf_op | source)
XLA Modules:
  0.0 85.1 jit_solution(5336101906976794937)
XLA Ops:
  0.0 84.4 %triangle.1 = bf16[7,56,128]{2,1,0:T(8,128)(2,1)S(1)} custom-call(bf16[7,56,128]{2,1,0:T(8,128)(2,1)} %pair_hbm.1, s32[7,56]{1,0:T(8,128)} %mask_hbm.1, bf16[2,128,512]{2,1,0:T(8,128)(2,1)} %wab_hbm.1, bf16[2,128,128]{2,1,0:T(8,128)(2,1)} %wg_hbm.1, bf16[2,128,128]{2,1,0:T(8,128)(2,1)} %wo_hbm.1), custom_call_target="tpu_custom_call" | custom-call | tf_op jit(solution)/shard_map/triangle/pallas_call | solution.py:389
  84.5 0.6 copy.7

commit v11 on v9

--- a/solution.py
+++ b/solution.py
@@ -264,8 +264,8 @@
         if u == 0:
             pl.semaphore_wait(barrier, NZ - 1 + 4 * NG - 1)
             push_dense()
+            push_rest()
             constants()
-            push_rest()
             ztok[...] = jnp.zeros_like(ztok)
             for r in range(ROWS):
                 ztok[slot_rows(r), :] = pair_ref[r].astype(F32)

time: 83.9 us -> 83.8 us (level)
  no operation moved by 1% of the time
where the time goes in v11:
time: 83.8 us; the launch traced here: 83.6 us
  Pallas kernels  82.9 us (99%)
    pallas_call x1, Pallas kernels, body(): pl.pallas_call(kernel, out_shape=pltpu.VMEM(pair.shape, pair.dtype), in_s...  82.9 us

profile of v11, /device:TPU:24, one launch (start us, length us, event | category | flops | bytes accessed | tf_op | source)
XLA Modules:
  0.0 83.6 jit_solution(6768918014784572868)
XLA Ops:
  0.0 82.9 %triangle.1 = bf16[7,56,128]{2,1,0:T(8,128)(2,1)S(1)} custom-call(bf16[7,56,128]{2,1,0:T(8,128)(2,1)} %pair_hbm.1, s32[7,56]{1,0:T(8,128)} %mask_hbm.1, bf16[2,128,512]{2,1,0:T(8,128)(2,1)} %wab_hbm.1, bf16[2,128,128]{2,1,0:T(8,128)(2,1)} %wg_hbm.1, bf16[2,128,128]{2,1,0:T(8,128)(2,1)} %wo_hbm.1), custom_call_target="tpu_custom_call" | custom-call | tf_op jit(solution)/shard_map/triangle/pallas_call | solution.py:386
  82.9 0.6 copy.7
